TPU v7x, 128 devices: a whole 4x4x4 slice. The times are simulated.
128 devices in a mesh: tm: 8 (over x, core), lata: 4 (over y), latb: 4 (over z).
Axes of the slice: x: 4, y: 4, z: 4, core: 2. Of those that a mesh axis runs over, the one named last changes fastest.
Arguments:
- images: float32 [32, 2048, 4096], P('tm', ('lata', 'latb')), may hold values from -24 to 24
- pair_order: int32 [512], replicated, may hold values from 0 to 511, each once
- legendre: bfloat16 [512, 1025, 2048], P(('tm', 'lata', 'latb')), may hold values from -0.125 to 0.125
Outputs:
- mode_series: float32 [512, 1025, 64], P(('tm', 'lata', 'latb'))
Inputs may be any that keep to these rules, and one draw needn't show every extreme that they name: `pair_order`: each pair appears in exactly one slot.
All inputs are finite; a program needn't handle non-finite values.
Results may differ from a plain program's by a relative error of at most 0.0029.
Values may be sent and summed in bfloat16 or wider, within the bound.
No kernel may reach another device: no remote copies, remote signals or barrier semaphores. Data moves between devices by JAX's collectives and lax.ppermute only.
A program may use at most 192 MiB of HBM per device.

v0:
```python
import math

import jax
import jax.numpy as jnp
from jax import lax
from jax.sharding import PartitionSpec as P


def shards(images, pair_order, legendre):
    local_images, local_rows, longitudes = images.shape
    slots_here = legendre.shape[0]
    row_count = legendre.shape[1]
    modes = 2 * pair_order.shape[0]
    largest = modes - 1
    bands = lax.axis_size("lata") * lax.axis_size("latb")
    blocks = lax.axis_size("tm")
    latitudes = local_rows * bands
    squares = jnp.sum(images * images, axis=(1, 2))
    totals = lax.psum(squares, ("lata", "latb"))
    power = jnp.sqrt(totals / (latitudes * longitudes) + 1e-06)
    mode_list = jnp.stack([pair_order, largest - pair_order], axis=1).reshape(-1)
    wave = jnp.arange(longitudes, dtype=jnp.int32)
    flat = images.reshape(local_images * local_rows, longitudes)
    phase = wave[:, None] * jnp.arange(modes, dtype=jnp.int32)[None, :] % longitudes
    angle = phase.astype(jnp.float32) * (2.0 * math.pi / longitudes)
    whole = jnp.dot(
        flat,
        jnp.stack([jnp.cos(angle), -jnp.sin(angle)], axis=-1).reshape(longitudes, -1)
        / math.sqrt(longitudes),
        precision=lax.Precision.HIGHEST,
        preferred_element_type=jnp.float32,
    )
    whole = whole.reshape(local_images * local_rows, modes, 2)
    spectrum = jnp.take(whole, mode_list, axis=1).reshape(local_images, local_rows, 2 * modes)
    spectrum = (spectrum / power[:, None, None]).astype(jnp.bfloat16)
    outgoing = jnp.transpose(spectrum, (2, 0, 1))
    arrived = lax.all_to_all(
        outgoing, ("tm", "lata", "latb"), split_axis=0, concat_axis=2, tiled=True
    )
    arrived = arrived.reshape(slots_here * 4, local_images, blocks, bands, local_rows)
    arrived = jnp.transpose(arrived, (0, 3, 4, 2, 1))
    series_len = blocks * local_images
    arrived = arrived.reshape(slots_here, 4, latitudes, series_len)
    arrived = jnp.transpose(arrived, (0, 2, 1, 3)).reshape(slots_here, latitudes, 4 * series_len)
    blocked = jnp.einsum("krj,kjc->krc", legendre, arrived, preferred_element_type=jnp.float32)
    device = lax.axis_index(("tm", "lata", "latb"))
    mine = lax.dynamic_slice_in_dim(pair_order, device * slots_here, slots_here)
    row_ids = jnp.arange(row_count, dtype=jnp.int32)
    keep = row_ids[None, :] < (largest + 1 - mine)[:, None]
    half = 2 * series_len
    return jnp.where(keep[:, :, None], blocked[:, :, :half], blocked[:, :, half:])


def solution(mesh):
    in_specs = (P("tm", ("lata", "latb"), None), P(), P(("tm", "lata", "latb"), None, None))
    out_specs = P(("tm", "lata", "latb"), None, None)
    return jax.shard_map(shards, mesh=mesh, in_specs=in_specs, out_specs=out_specs, check_vma=False)
```

profile of v0, /device:TPU:1, one launch (start us, length us, event | category | flops | bytes accessed | tf_op | source)
XLA Modules:
  0.0 385.4 jit_solution(9972957730450870643)
XLA Ops:
  0.0 67.4 %sine_negate_fusion = (f32[4096,1024,1]{1,0,2:T(8,128)}, f32[4096,1024,1]{1,0,2:T(8,128)}) fusion(), kind=kLoop, calls=%fused_computation.10 | loop fusion | flops 62914560 | bytes 33554432 | tf_op jit(solution)/shard_map/neg | solution.py:28
  67.4 0.0 copy-done
  67.4 0.7 multiply_reduce_fusion
  68.1 0.0 copy-done.2
  68.1 0.1 copy.32
  68.2 0.2 reshape.162
  68.4 0.8 reshape.159
  69.2 35.8 %psum.7 = f32[4]{0:T(128)S(1)} all-reduce(f32[4]{0:T(128)S(1)} %multiply_reduce_fusion), channel_id=1, replica_groups=mesh['tm'=8,'lata'=4,'latb'=4] {'lata','latb'}, use_global_device_ids=true, to_apply=%region_1.0 | all-reduce | flops 4 | bytes 32 | tf_op jit(solution)/shard_map/psum | solution.py:19
  105.0 0.6 add_sqrt_fusion
  105.5 24.6 %maximum_multiply_fusion = f32[4096,1024,2]{1,0,2:T(8,128)} fusion(f32[4096,1024,1]{1,0,2:T(8,128)} %get-tuple-element.5, f32[4096,1024,1]{1,0,2:T(8,128)} %get-tuple-element.6), kind=kLoop, calls=%fused_computation.1 | loop fusion | flops 16777216 | bytes 67108864 | tf_op jit(solution)/shard_map/div | solution.py:28
  130.1 49.4 %copy.33 = f32[4096,1024,2]{0,2,1:T(2,128)} copy(f32[4096,1024,2]{1,0,2:T(8,128)} %maximum_multiply_fusion) | data formatting | bytes 67108864 | tf_op jit(solution)/shard_map/div | solution.py:28
  179.5 39.8 %div.21 = f32[4096,2048]{0,1:T(8,128)} reshape(f32[4096,1024,2]{0,2,1:T(2,128)} %copy.33) | data formatting | bytes 67108864 | tf_op jit(solution)/shard_map/div | solution.py:28
  219.3 60.3 %convolution_bitcast_fusion = f32[512,2048]{0,1:T(8,128)} fusion(f32[4096,2048]{0,1:T(8,128)} %div.21, f32[512,4096]{1,0:T(8,128)} %bitcast.35), kind=kOutput, calls=%fused_computation.19 | convolution fusion | flops 51539607552 | bytes 46137344 | tf_op jit(solution)/shard_map/dot_general | solution.py:26
  279.6 5.8 %reshape.161 = f32[512,1024,2]{0,2,1:T(2,128)} reshape(f32[512,2048]{0,1:T(8,128)} %convolution_bitcast_fusion) | data formatting | bytes 8388608 | tf_op jit(solution)/shard_map/reshape | solution.py:33
  285.4 0.0 copy-start.1
  285.4 0.0 copy-start.3
  285.4 13.8 %gather_fusion = f32[1024,512,2]{1,2,0:T(2,128)} fusion(f32[512,1024,2]{0,2,1:T(2,128)} %reshape.161, s32[1024]{0:T(1024)S(1)} %broadcast_clamp_fusion), kind=kCustom, calls=%fused_computation | custom fusion | bytes 8392704 | tf_op jit(solution)/shard_map/jit(_take)/gather | solution.py:34
  299.2 7.0 %gather.7 = f32[4,128,2048]{1,0,2:T(4,128)} reshape(f32[512,1024,2]{0,2,1:T(2,128)} %bitcast.34) | data formatting | bytes 8388608 | tf_op jit(solution)/shard_map/jit(_take)/gather | solution.py:34
  306.2 0.2 broadcast_in_dim.29
  306.4 0.3 broadcast_in_dim.30
  306.8 0.0 copy-done.3
  306.8 11.4 %fusion.13 = bf16[2048,4,128]{2,1,0:T(4,128)(2,1)} fusion(f32[4]{0:T(128)S(1)} %copy-done.3, f32[4,128,2048]{1,0,2:T(4,128)} %gather.7, pred[2048]{0:T(1024)(128)(4,1)S(1)} %broadcast_in_dim.30), kind=kLoop, calls=%fused_computation.21 | loop fusion | flops 3145728 | bytes 6293520 | tf_op jit(solution)/shard_map/transpose | solution.py:36
  318.1 11.7 %all-to-all-start = ((bf16[2048,4,128]{2,1,0:T(4,128)(2,1)}), bf16[2048,4,128]{2,1,0:T(4,128)(2,1)S(1)}, u32[]{:S(2)}, u32[]{:S(2)}) async-start(bf16[2048,4,128]{2,1,0:T(4,128)(2,1)} %fusion.13), calls=%async_computation | async-start | bytes 4194304 | tf_op jit(solution)/shard_map/all_to_all | solution.py:37
  329.9 0.8 dynamic-slice_subtract_fusion
  330.6 0.1 iota_compare_fusion
  330.7 28.6 %all-to-all-done = bf16[2048,4,128]{2,1,0:T(4,128)(2,1)S(1)} async-done(((bf16[2048,4,128]{2,1,0:T(4,128)(2,1)}), bf16[2048,4,128]{2,1,0:T(4,128)(2,1)S(1)}, u32[]{:S(2)}, u32[]{:S(2)}) %all-to-all-start) | async-done | bytes 2097184 | tf_op jit(solution)/shard_map/all_to_all | solution.py:37
  359.3 0.3 copy.35
  359.6 0.6 copy.37
  360.2 2.3 reshape.164
  362.5 17.6 %fusion.10 = f32[4,1025,128]{2,1,0:T(8,128)S(1)} fusion(bf16[4,2048,128]{1,2,0:T(8,128)(2,1)} %bitcast.37, bf16[4,1025,2048]{2,0,1:T(4,128)(2,1)} %param.5), kind=kOutput, calls=%fused_computation.18 | convolution fusion | flops 2149580800 | bytes 20989952 | tf_op jit(solution)/shard_map/krj,kjc->krc/dot_general | solution.py:45
  380.1 2.6 slice_select_fusion
  382.7 2.8 copy.40
  (8 shorter events, 0.0 us)
Async XLA Ops:
  0.0 67.4 %copy-start = (f32[4,128,4096]{2,1,0:T(8,128)S(1)}, f32[4,128,4096]{2,1,0:T(8,128)}, u32[]{:S(2)}) copy-start(f32[4,128,4096]{2,1,0:T(8,128)} %param.3) | copy-start | bytes 25165828
  0.0 68.1 %copy-start.2 = (s32[512]{0:T(512)S(1)}, s32[512]{0:T(512)}, u32[]{:S(2)}) copy-start(s32[512]{0:T(512)} %param.4) | copy-start | bytes 6148
  285.4 20.8 %copy-start.1 = (s32[1024]{0:T(1024)S(1)}, s32[1024]{0:T(1024)}, u32[]{:S(2)}) copy-start(s32[1024]{0:T(1024)} %reshape.159) | copy-start | bytes 12292
  285.4 21.3 %copy-start.3 = (f32[4]{0:T(128)S(1)}, f32[4]{0:T(128)}, u32[]{:S(2)}) copy-start(f32[4]{0:T(128)} %add_sqrt_fusion) | copy-start | bytes 52
  318.1 41.2 %all-to-all-start = ((bf16[2048,4,128]{2,1,0:T(4,128)(2,1)}), bf16[2048,4,128]{2,1,0:T(4,128)(2,1)S(1)}, u32[]{:S(2)}, u32[]{:S(2)}) async-start(bf16[2048,4,128]{2,1,0:T(4,128)(2,1)} %fusion.13), calls=%async_computation | async-start | bytes 4194304 | tf_op jit(solution)/shard_map/all_to_all | solution.py:37
where the time goes:
time: 388 us; the launch traced here: 385 us
  local copies, waits for them, and re-layouts  123 us (32%)
  other arithmetic  108 us (28%)
  matrix products  77.9 us (20%)
  blocking collectives  35.8 us (9%)
  waiting for transfers between devices  28.6 us (7%)
  starting transfers between devices  11.7 us (3%)
    div x2, local copies, waits for them, and re-layouts, shards(): jnp.stack([jnp.cos(angle), -jnp.sin(angle)], axis=-1)  89.2 us
    neg x1, other arithmetic, shards(): -jnp.sin(angle)  67.4 us
    dot_general x1, matrix products, shards(): jnp.dot(flat, jnp.stack([jnp.cos(angle), -jnp.sin(angle)], axis=-1).resha...  60.3 us
    psum x1, blocking collectives, shards(): totals = lax.psum(squares, ('lata', 'latb'))  35.8 us
    all_to_all x1, waiting for transfers between devices, shards(): lax.all_to_all(outgoing, ('tm', 'lata', 'latb'), split_axis=0, concat_axi...  28.6 us
    div x1, other arithmetic, shards(): jnp.stack([jnp.cos(angle), -jnp.sin(angle)], axis=-1)  24.6 us
    gather x2, local copies, waits for them, and re-layouts, shards(): jnp.take(whole, mode_list, axis=1)  20.8 us
    dot_general x1, matrix products, shards(): jnp.einsum('krj,kjc->krc', legendre, arrived, preferred_element_type=jnp....  17.6 us
  transfers between devices with their start and end apart: 1, of which 1 were waited for; matrix products, arithmetic and copies ran while one was open for 0% of the time, Pallas kernels for 0%

commit v1 on v0

v1 whole, which is shorter than its diff:
```python
import math

import jax
import jax.numpy as jnp
import numpy as np
from jax import lax
from jax.experimental import pallas as pl
from jax.experimental.pallas import tpu as pltpu
from jax.sharding import PartitionSpec as P

NT = (((1,), (1,)), ((), ()))


def tables():
    q = np.arange(32)
    k = np.arange(256)

    def rows(freq, conj):
        angle = 2.0 * np.pi / 4096.0 * ((freq[:, None] * k[None, :]) % 4096)
        c, s = np.cos(angle) / 64.0, np.sin(angle) / 64.0
        re = np.concatenate([c, s], 1)
        im = np.concatenate([-s, c], 1)
        return re, (-im if conj else im)

    def real_rows(freq, second):
        angle = 2.0 * np.pi / 4096.0 * ((freq[:, None] * k[None, :]) % 4096)
        c, s = np.cos(angle) / 64.0, np.sin(angle) / 64.0
        zero = np.zeros_like(c)
        pair = (zero, c), (zero, -s)
        if not second:
            pair = (c, zero), (-s, zero)
        return [np.concatenate(p, 1) for p in pair]

    first, other = [], []
    for high in (0, 1):
        n = 63 - q if high else q
        first += list(real_rows(16 * n, False))
        other += list(rows(16 * n, False))
    for high in (0, 1):
        n = 63 - q if high else q
        first += list(real_rows(8 + 16 * n, True))
        other += list(rows(-16 * (n + 1), True))
    whole = np.stack([np.concatenate(first, 0), np.concatenate(other, 0)]).astype(np.float32)
    hi = whole.astype(jnp.bfloat16)
    lo = (whole - hi.astype(np.float32)).astype(jnp.bfloat16)
    angle = 2.0 * np.pi / 4096.0 * (np.arange(8)[:, None] * k[None, :])
    twiddle = np.stack([np.cos(angle), -np.sin(angle)], 1).reshape(16, 256).astype(np.float32)
    return np.concatenate([hi, lo], 2), twiddle


def rfft(x):
    n = len(x)
    if n == 2:
        return [(x[0] + x[1], None), (x[0] - x[1], None)]
    even, odd = rfft(x[0::2]), rfft(x[1::2])
    out = [None] * (n // 2 + 1)
    out[0] = (even[0][0] + odd[0][0], None)
    out[n // 2] = (even[0][0] - odd[0][0], None)
    for b in range(1, n // 4 + 1):
        er, ei = even[b]
        dr, di = odd[b]
        if 4 * b == n:
            out[b] = (er, -dr)
            continue
        c, s = math.cos(2 * math.pi * b / n), -math.sin(2 * math.pi * b / n)
        if 8 * b == n:
            tr, ti = (dr + di) * c, (di - dr) * c
        else:
            tr, ti = dr * c - di * s, dr * s + di * c
        out[b] = (er + tr, ei + ti)
        out[n // 2 - b] = (er - tr, ti - ei)
    return out


def fourier_kernel(order_ref, image_ref, matrix_ref, twiddle_ref, out_ref, square_ref, z_ref, natural_ref):
    step = pl.program_id(0)
    for t in range(2):

        def rows(i, total, t=t):
            at = pl.ds(pl.multiple_of(i * 16, 16), 16)
            to = pl.ds(pl.multiple_of(t * 128 + i * 16, 16), 16)
            for half in range(2):
                lanes = slice(half * 128, half * 128 + 128)
                x = [image_ref[t, at, b * 256 + half * 128 : b * 256 + half * 128 + 128] for b in range(16)]
                for v in x:
                    total = total + v * v
                bins = rfft(x)

                def put(g, part, value):
                    hi = value.astype(jnp.bfloat16)
                    lo = (value - hi.astype(jnp.float32)).astype(jnp.bfloat16)
                    z_ref[g, to, part * 256 + half * 128 : part * 256 + half * 128 + 128] = hi
                    z_ref[g, to, 512 + part * 256 + half * 128 : 512 + part * 256 + half * 128 + 128] = lo

                put(0, 0, bins[0][0])
                put(0, 1, bins[8][0])
                for g in range(1, 8):
                    re, im = bins[g]
                    c = twiddle_ref[2 * g : 2 * g + 1, lanes]
                    s = twiddle_ref[2 * g + 1 : 2 * g + 2, lanes]
                    put(g, 0, re * c - im * s)
                    put(g, 1, re * s + im * c)
            return total

        total = lax.fori_loop(0, 8, rows, jnp.zeros((16, 128), jnp.float32))
        square_ref[pl.ds(step * 2 + t, 1), :] = jnp.sum(total, axis=0, keepdims=True)

    for g in range(8):
        kind = 0 if g == 0 else 1
        got = lax.dot_general(matrix_ref[kind, :, :512], z_ref[g, :, :512], NT, preferred_element_type=jnp.float32)
        got += lax.dot_general(matrix_ref[kind, :, :512], z_ref[g, :, 512:], NT, preferred_element_type=jnp.float32)
        got += lax.dot_general(matrix_ref[kind, :, 512:], z_ref[g, :, :512], NT, preferred_element_type=jnp.float32)
        for which, residue in enumerate((g, 8 if g == 0 else 16 - g)):
            for w in range(2):
                slot = 15 - residue if w else residue
                for c in range(2):
                    block = got[((which * 2 + w) * 2 + c) * 32 : ((which * 2 + w) * 2 + c) * 32 + 32]
                    for t in range(2):
                        natural_ref[pl.ds(slot * 512 + w * 8 + c * 4 + step * 2 + t, 32, stride=16), :] = block[:, t * 128 : t * 128 + 128]

    @pl.when(step == 1)
    def _():
        def place(i, carry):
            for u in range(8):
                s = i * 8 + u
                p = order_ref[s]
                at = pl.multiple_of((p % 16) * 512 + (p // 16) * 16, 16)
                out_ref[pl.ds(pl.multiple_of(s * 16, 16), 16), :] = natural_ref[pl.ds(at, 16), :].astype(jnp.bfloat16)
            return carry

        lax.fori_loop(0, 64, place, 0)


def fourier(pair_order, images, matrix, twiddle):
    return pl.pallas_call(
        fourier_kernel,
        grid=(2,),
        out_shape=(jax.ShapeDtypeStruct((8192, 128), jnp.bfloat16), jax.ShapeDtypeStruct((4, 128), jnp.float32)),
        in_specs=[
            pl.BlockSpec(memory_space=pltpu.SMEM),
            pl.BlockSpec((2, 128, 4096), lambda i: (i, 0, 0)),
            pl.BlockSpec((2, 256, 1024), lambda i: (0, 0, 0)),
            pl.BlockSpec((16, 256), lambda i: (0, 0)),
        ],
        out_specs=(pl.BlockSpec((8192, 128), lambda i: (0, 0)), pl.BlockSpec((4, 128), lambda i: (0, 0))),
        scratch_shapes=[pltpu.VMEM((8, 256, 1024), jnp.bfloat16), pltpu.VMEM((8192, 128), jnp.float32)],
        compiler_params=pltpu.CompilerParams(vmem_limit_bytes=60 << 20),
        cost_estimate=pl.CostEstimate(flops=4 << 30, bytes_accessed=12 << 20, transcendentals=0),
    )(pair_order, images, matrix, twiddle)


def legendre_kernel(mine_ref, got_ref, mix_ref, scale_ref, legendre_ref, out_ref, column_ref):
    slot = pl.program_id(0)
    for band in range(16):
        for block in range(8):
            column_ref[block * 16 : block * 16 + 16, band * 128 : band * 128 + 128] = got_ref[
                block * 16 + band, pl.ds(pl.multiple_of(slot * 16, 16), 16), :
            ]
    columns = jnp.dot(mix_ref[...], column_ref[...], preferred_element_type=jnp.float32).astype(jnp.bfloat16)
    block = lax.dot_general(legendre_ref[0], columns, NT, preferred_element_type=jnp.float32)
    row = lax.broadcasted_iota(jnp.int32, (block.shape[0], 64), 0)
    kept = jnp.where(row <= 1023 - mine_ref[slot], block[:, :64], block[:, 64:])
    out_ref[0] = jnp.transpose(kept) * scale_ref[...]


def associated(mine, got, mix, scale, legendre):
    return pl.pallas_call(
        legendre_kernel,
        grid=(4,),
        out_shape=jax.ShapeDtypeStruct((4, 64, 1025), jnp.float32),
        in_specs=[
            pl.BlockSpec(memory_space=pltpu.SMEM),
            pl.BlockSpec((128, 64, 128), lambda i: (0, 0, 0)),
            pl.BlockSpec((128, 128), lambda i: (0, 0)),
            pl.BlockSpec((64, 1), lambda i: (0, 0)),
            pl.BlockSpec((1, 1025, 2048), lambda i: (i, 0, 0)),
        ],
        out_specs=pl.BlockSpec((1, 64, 1025), lambda i: (i, 0, 0)),
        scratch_shapes=[pltpu.VMEM((128, 2048), jnp.bfloat16)],
        compiler_params=pltpu.CompilerParams(vmem_limit_bytes=56 << 20),
        cost_estimate=pl.CostEstimate(flops=4 << 30, bytes_accessed=22 << 20, transcendentals=0),
    )(mine, got, mix, scale, legendre)


def shifted(value, axis, size, by):
    return lax.ppermute(value, axis, [(i, (i + by) % size) for i in range(size)])


def shards(images, pair_order, legendre):
    matrix, twiddle = tables()
    message, squares = fourier(pair_order, images, jnp.asarray(matrix), jnp.asarray(twiddle))
    axes = ("tm", "lata", "latb")
    got = lax.all_to_all(message.reshape(128, 64, 128), axes, split_axis=0, concat_axis=0, tiled=True)
    total = jnp.sum(squares, axis=1)
    for axis in ("latb", "lata"):
        total = total + sum(shifted(total, axis, 4, by) for by in range(1, 4))
    own = jnp.where(jnp.arange(8)[:, None] == lax.axis_index("tm"), total[None, :], 0.0)
    every = own + sum(shifted(own, "tm", 8, by) for by in range(1, 8))
    power = jnp.sqrt(every.reshape(32) / 8388608.0 + 1e-6)
    scale = jnp.tile(1.0 / power, 2).reshape(64, 1)
    mine = lax.dynamic_slice_in_dim(pair_order, lax.axis_index(axes) * 4, 4)
    mix = np.zeros((128, 128), np.float32)
    for block in range(8):
        for wc in range(4):
            for t in range(4):
                mix[wc * 32 + block * 4 + t, block * 16 + wc * 4 + t] = 1.0
    series = associated(mine, got, jnp.asarray(mix, jnp.bfloat16), scale, legendre)
    return jnp.transpose(series, (0, 2, 1))


def solution(mesh):
    in_specs = (P("tm", ("lata", "latb"), None), P(), P(("tm", "lata", "latb"), None, None))
    out_specs = P(("tm", "lata", "latb"), None, None)
    return jax.shard_map(shards, mesh=mesh, in_specs=in_specs, out_specs=out_specs, check_vma=False)
```

time: 388 us -> 87.4 us (0.23)
  other arithmetic: 108 us -> 0.97 us
  local copies, waits for them, and re-layouts: 123 us -> 18.9 us
  matrix products: 77.9 us -> 0 us
  blocking collectives: 35.8 us -> 0 us
  Pallas kernels: 0 us -> 28.5 us
  waiting for transfers between devices: 28.6 us -> 5.47 us
  starting transfers between devices: 11.7 us -> 33.1 us
    div x2 -> x0, local copies, waits for them, and re-layouts: 89.2 us -> none  [shards(): jnp.stack([jnp.cos(angle), -jnp.sin(angle)], axis=-1)]
    dot_general x2 -> x0, matrix products: 77.9 us -> none  [the longest x1 60.3 us: shards(): jnp.dot(flat, jnp.stack([jnp.cos(angle), -jnp.sin(angle)], axis=-1).resha...]
    neg x1 -> x0, other arithmetic: 67.4 us -> none  [shards(): -jnp.sin(angle)]
    psum x1 -> x0, blocking collectives: 35.8 us -> none  [shards(): totals = lax.psum(squares, ('lata', 'latb'))]
    all_to_all x1, waiting for transfers between devices: 28.6 us -> 0.01 us  [shards(): lax.all_to_all(message.reshape(128, 64, 128), axes, split_axis=0, concat_...]
    pallas_call x0 -> x2, Pallas kernels: none -> 28.5 us  [the longest x1 16.9 us: fourier(): pl.pallas_call(fourier_kernel, grid=(2,), out_shape=(jax.ShapeDtypeStruct...]
    div x1 -> x0, other arithmetic: 24.6 us -> none  [shards(): jnp.stack([jnp.cos(angle), -jnp.sin(angle)], axis=-1)]
    ppermute x0 -> x13, starting transfers between devices: none -> 21.6 us  [shifted(): lax.ppermute(value, axis, [(i, (i + by) % size) for i in range(size)])]
  transfers between devices with their start and end apart: 1 -> 14, of which waited for: 1 -> 4; matrix products, arithmetic and copies ran while one was open for 0% -> 21% of each run, Pallas kernels for 0% -> 0%
where the time goes in v1:
time: 87.4 us; the launch traced here: 87 us
  starting transfers between devices  33.1 us (38%)
  Pallas kernels  28.5 us (33%)
  local copies, waits for them, and re-layouts  18.9 us (22%)
  waiting for transfers between devices  5.47 us (6%)
  other arithmetic  0.97 us (1%)
    ppermute x13, starting transfers between devices, shifted(): lax.ppermute(value, axis, [(i, (i + by) % size) for i in range(size)])  21.6 us
    pallas_call x1, Pallas kernels, fourier(): pl.pallas_call(fourier_kernel, grid=(2,), out_shape=(jax.ShapeDtypeStruct...  16.9 us
    unnamed x3, local copies, waits for them, and re-layouts  16.8 us
    pallas_call x1, Pallas kernels, associated(): pl.pallas_call(legendre_kernel, grid=(4,), out_shape=jax.ShapeDtypeStruct...  11.6 us
    all_to_all x1, starting transfers between devices, shards(): lax.all_to_all(message.reshape(128, 64, 128), axes, split_axis=0, concat_...  11.5 us
    ppermute x13, waiting for transfers between devices, shifted(): lax.ppermute(value, axis, [(i, (i + by) % size) for i in range(size)])  5.47 us
  transfers between devices with their start and end apart: 14, of which 4 were waited for; matrix products, arithmetic and copies ran while one was open for 21% of the time, Pallas kernels for 0%

profile of v1, /device:TPU:1, one launch (start us, length us, event | category | flops | bytes accessed | tf_op | source)
XLA Modules:
  0.0 87.0 jit_solution(7710547858545722178)
XLA Ops:
  0.0 16.9 %shard_map.64 = (bf16[8192,128]{1,0:T(8,128)(2,1)}, f32[4,128]{1,0:T(4,128)}) custom-call(s32[512]{0:T(512)} %order_ref.1, f32[4,128,4096]{2,1,0:T(8,128)} %image_ref.1, bf16[2,256,1024]{2,1,0:T(8,128)(2,1)} %constant.35.clone.matrix_ref, f32[16,256]{1,0:T(8,128)} %constant.36.clone.twiddle_ref), custom_call_target="tpu_custom_call" | custom-call | flops 4294967296 | bytes 12582912 | tf_op jit(solution)/shard_map/pallas_call | solution.py:135
  16.9 11.5 %all-to-all-start = ((bf16[128,64,128]{2,1,0:T(8,128)(2,1)}), bf16[128,64,128]{2,1,0:T(8,128)(2,1)S(1)}, u32[]{:S(2)}, u32[]{:S(2)}) async-start(bf16[128,64,128]{2,1,0:T(8,128)(2,1)} %bitcast.2), calls=%async_computation | async-start | bytes 4194304 | tf_op jit(solution)/shard_map/all_to_all | solution.py:193
  28.4 0.8 reduce_sum.9
  29.2 3.3 %collective-permute-start.2 = (f32[4]{0:T(128)S(1)}, f32[4]{0:T(128)S(1)}, u32[]{:S(2)}, u32[]{:S(2)}) collective-permute-start(f32[4]{0:T(128)S(1)} %reduce_sum.9), channel_id=1, source_target_pairs={{0,3},{1,0},{2,1},{3,2},{4,7},{5,4},{6,5},{7,6},{8,11},{9,8},{10,9... | collective-permute-start | bytes 56 | tf_op jit(solution)/shard_map/ppermute | solution.py:186
  32.5 0.1 collective-permute-start.1
  32.6 0.8 collective-permute-start
  33.4 1.3 %dynamic_slice.3.mine_ref = s32[4]{0:T(128)} dynamic-slice(s32[512]{0:T(512)} %order_ref.1, s32[]{:T(128)S(6)} %select_n.7), dynamic_slice_sizes={4} | dynamic-slice | bytes 36 | tf_op jit(solution)/shard_map/dynamic_slice | solution.py:201
  34.7 15.5 %copy.10.legendre_ref = bf16[4,1025,2048]{2,1,0:T(8,128)(2,1)} copy(bf16[4,1025,2048]{2,0,1:T(4,128)(2,1)} %param.8) | data formatting | bytes 33587200 | tf_op args[2]
  50.2 0.0 collective-permute-done.2
  50.2 0.0 collective-permute-done.1
  50.3 3.1 %collective-permute-start.5 = (f32[4]{0:T(128)S(1)}, f32[4]{0:T(128)S(1)}, u32[]{:S(2)}, u32[]{:S(2)}) collective-permute-start(f32[4]{0:T(128)S(1)} %add_add_fusion.1), channel_id=1, source_target_pairs={{0,12},{4,0},{8,4},{12,8},{1,13},{5,1},{9,5},{13,9},{2,14},{6,2},{... | collective-permute-start | bytes 56 | tf_op jit(solution)/shard_map/ppermute | solution.py:186
  53.4 0.0 collective-permute-start.4
  53.4 0.7 collective-permute-start.3
  54.1 0.1 collective-permute-done.5
  54.1 3.5 %collective-permute-done.4 = f32[4]{0:T(128)S(1)} collective-permute-done((f32[4]{0:T(128)S(1)}, f32[4]{0:T(128)S(1)}, u32[]{:S(2)}, u32[]{:S(2)}) %collective-permute-start.4) | collective-permute-done | bytes 48 | tf_op jit(solution)/shard_map/ppermute | solution.py:186
  57.6 0.1 broadcast_select_fusion
  57.7 2.3 %collective-permute-start.12 = (f32[8,4]{1,0:T(8,128)S(1)}, f32[8,4]{1,0:T(8,128)S(1)}, u32[]{:S(2)}, u32[]{:S(2)}) collective-permute-start(f32[8,4]{1,0:T(8,128)S(1)} %broadcast_select_fusion), channel_id=1, source_target_pairs={{0,112},{16,0},{32,16},{48,32},{64,48},{80,64},{96,80},{112,96},{1... | collective-permute-start | bytes 392 | tf_op jit(solution)/shard_map/ppermute | solution.py:186
  60.0 5.8 %collective-permute-start.11 = (f32[8,4]{1,0:T(8,128)S(1)}, f32[8,4]{1,0:T(8,128)S(1)}, u32[]{:S(2)}, u32[]{:S(2)}) collective-permute-start(f32[8,4]{1,0:T(8,128)S(1)} %broadcast_select_fusion), channel_id=1, source_target_pairs={{0,96},{16,112},{32,0},{48,16},{64,32},{80,48},{96,64},{112,80},{1... | collective-permute-start | bytes 392 | tf_op jit(solution)/shard_map/ppermute | solution.py:186
  65.8 0.0 collective-permute-start.10
  65.8 1.4 %collective-permute-start.9 = (f32[8,4]{1,0:T(8,128)S(1)}, f32[8,4]{1,0:T(8,128)S(1)}, u32[]{:S(2)}, u32[]{:S(2)}) collective-permute-start(f32[8,4]{1,0:T(8,128)S(1)} %broadcast_select_fusion), channel_id=1, source_target_pairs={{0,64},{16,80},{32,96},{48,112},{64,0},{80,16},{96,32},{112,48},{1... | collective-permute-start | bytes 392 | tf_op jit(solution)/shard_map/ppermute | solution.py:186
  67.2 2.0 %collective-permute-start.8 = (f32[8,4]{1,0:T(8,128)S(1)}, f32[8,4]{1,0:T(8,128)S(1)}, u32[]{:S(2)}, u32[]{:S(2)}) collective-permute-start(f32[8,4]{1,0:T(8,128)S(1)} %broadcast_select_fusion), channel_id=1, source_target_pairs={{0,48},{16,64},{32,80},{48,96},{64,112},{80,0},{96,16},{112,32},{1... | collective-permute-start | bytes 392 | tf_op jit(solution)/shard_map/ppermute | solution.py:186
  69.2 0.0 collective-permute-done.12
  69.2 0.7 collective-permute-start.7
  69.9 0.0 collective-permute-done.11
  69.9 1.4 %collective-permute-start.6 = (f32[8,4]{1,0:T(8,128)S(1)}, f32[8,4]{1,0:T(8,128)S(1)}, u32[]{:S(2)}, u32[]{:S(2)}) collective-permute-start(f32[8,4]{1,0:T(8,128)S(1)} %broadcast_select_fusion), channel_id=1, source_target_pairs={{0,16},{16,32},{32,48},{48,64},{64,80},{80,96},{96,112},{112,0},{1... | collective-permute-start | bytes 392 | tf_op jit(solution)/shard_map/ppermute | solution.py:186
  71.3 0.2 collective-permute-done.8
  71.5 1.7 %collective-permute-done.7 = f32[8,4]{1,0:T(8,128)S(1)} collective-permute-done((f32[8,4]{1,0:T(8,128)S(1)}, f32[8,4]{1,0:T(8,128)S(1)}, u32[]{:S(2)}, u32[]{:S(2)}) %collective-permute-start.7) | collective-permute-done | bytes 160 | tf_op jit(solution)/shard_map/ppermute | solution.py:186
  73.2 0.1 add_rsqrt_fusion
  73.3 0.1 sqrt.6
  73.4 0.7 reshape_tile.4.scale_ref
  74.1 1.3 %copy-done = bf16[128,64,128]{2,1,0:T(8,128)(2,1)} copy-done((bf16[128,64,128]{2,1,0:T(8,128)(2,1)}, bf16[128,64,128]{2,1,0:T(8,128)(2,1)S(1)}, u32[]{:S(2)}) %copy-start) | copy-done | bytes 2097176
  75.4 11.6 %shard_map.65 = f32[4,64,1025]{2,1,0:T(8,128)} custom-call(s32[4]{0:T(128)} %dynamic_slice.3.mine_ref, bf16[128,64,128]{2,1,0:T(8,128)(2,1)} %copy-done, bf16[128,128]{1,0:T(8,128)(2,1)} %constant.37.clone.mix_ref, f32[64,1]{1,0:T(8,128)} %reshape_tile.4.scale_ref, bf16[4,1025,2048]{2,1,0:T(8,128)(2,1)} %copy.10.legendre_ref), custom_call_target="tpu_custom_call" | custom-call | flops 4294967296 | bytes 23068672 | tf_op jit(solution)/shard_map/pallas_call | solution.py:167
  (11 shorter events, 0.0 us)
Async XLA Ops:
  16.9 57.2 %all-to-all-start = ((bf16[128,64,128]{2,1,0:T(8,128)(2,1)}), bf16[128,64,128]{2,1,0:T(8,128)(2,1)S(1)}, u32[]{:S(2)}, u32[]{:S(2)}) async-start(bf16[128,64,128]{2,1,0:T(8,128)(2,1)} %bitcast.2), calls=%async_computation | async-start | bytes 4194304 | tf_op jit(solution)/shard_map/all_to_all | solution.py:193
  29.2 21.0 %collective-permute-start.2 = (f32[4]{0:T(128)S(1)}, f32[4]{0:T(128)S(1)}, u32[]{:S(2)}, u32[]{:S(2)}) collective-permute-start(f32[4]{0:T(128)S(1)} %reduce_sum.9), channel_id=1, source_target_pairs={{0,3},{1,0},{2,1},{3,2},{4,7},{5,4},{6,5},{7,6},{8,11},{9,8},{10,9... | collective-permute-start | bytes 56 | tf_op jit(solution)/shard_map/ppermute | solution.py:186
  32.5 17.7 %collective-permute-start.1 = (f32[4]{0:T(128)S(1)}, f32[4]{0:T(128)S(1)}, u32[]{:S(2)}, u32[]{:S(2)}) collective-permute-start(f32[4]{0:T(128)S(1)} %reduce_sum.9), channel_id=1, source_target_pairs={{0,2},{1,3},{2,0},{3,1},{4,6},{5,7},{6,4},{7,5},{8,10},{9,11},{10,... | collective-permute-start | bytes 56 | tf_op jit(solution)/shard_map/ppermute | solution.py:186
  32.6 17.6 %collective-permute-start = (f32[4]{0:T(128)S(1)}, f32[4]{0:T(128)S(1)}, u32[]{:S(2)}, u32[]{:S(2)}) collective-permute-start(f32[4]{0:T(128)S(1)} %reduce_sum.9), channel_id=1, source_target_pairs={{0,1},{1,2},{2,3},{3,0},{4,5},{5,6},{6,7},{7,4},{8,9},{9,10},{10,1... | collective-permute-start | bytes 56 | tf_op jit(solution)/shard_map/ppermute | solution.py:186
  50.3 3.9 %collective-permute-start.5 = (f32[4]{0:T(128)S(1)}, f32[4]{0:T(128)S(1)}, u32[]{:S(2)}, u32[]{:S(2)}) collective-permute-start(f32[4]{0:T(128)S(1)} %add_add_fusion.1), channel_id=1, source_target_pairs={{0,12},{4,0},{8,4},{12,8},{1,13},{5,1},{9,5},{13,9},{2,14},{6,2},{... | collective-permute-start | bytes 56 | tf_op jit(solution)/shard_map/ppermute | solution.py:186
  53.4 4.2 %collective-permute-start.4 = (f32[4]{0:T(128)S(1)}, f32[4]{0:T(128)S(1)}, u32[]{:S(2)}, u32[]{:S(2)}) collective-permute-start(f32[4]{0:T(128)S(1)} %add_add_fusion.1), channel_id=1, source_target_pairs={{0,8},{4,12},{8,0},{12,4},{1,9},{5,13},{9,1},{13,5},{2,10},{6,14},... | collective-permute-start | bytes 56 | tf_op jit(solution)/shard_map/ppermute | solution.py:186
  53.4 4.2 %collective-permute-start.3 = (f32[4]{0:T(128)S(1)}, f32[4]{0:T(128)S(1)}, u32[]{:S(2)}, u32[]{:S(2)}) collective-permute-start(f32[4]{0:T(128)S(1)} %add_add_fusion.1), channel_id=1, source_target_pairs={{0,4},{4,8},{8,12},{12,0},{1,5},{5,9},{9,13},{13,1},{2,6},{6,10},{... | collective-permute-start | bytes 56 | tf_op jit(solution)/shard_map/ppermute | solution.py:186
  57.7 11.6 %collective-permute-start.12 = (f32[8,4]{1,0:T(8,128)S(1)}, f32[8,4]{1,0:T(8,128)S(1)}, u32[]{:S(2)}, u32[]{:S(2)}) collective-permute-start(f32[8,4]{1,0:T(8,128)S(1)} %broadcast_select_fusion), channel_id=1, source_target_pairs={{0,112},{16,0},{32,16},{48,32},{64,48},{80,64},{96,80},{112,96},{1... | collective-permute-start | bytes 392 | tf_op jit(solution)/shard_map/ppermute | solution.py:186
  60.0 9.9 %collective-permute-start.11 = (f32[8,4]{1,0:T(8,128)S(1)}, f32[8,4]{1,0:T(8,128)S(1)}, u32[]{:S(2)}, u32[]{:S(2)}) collective-permute-start(f32[8,4]{1,0:T(8,128)S(1)} %broadcast_select_fusion), channel_id=1, source_target_pairs={{0,96},{16,112},{32,0},{48,16},{64,32},{80,48},{96,64},{112,80},{1... | collective-permute-start | bytes 392 | tf_op jit(solution)/shard_map/ppermute | solution.py:186
  65.8 5.5 %collective-permute-start.10 = (f32[8,4]{1,0:T(8,128)S(1)}, f32[8,4]{1,0:T(8,128)S(1)}, u32[]{:S(2)}, u32[]{:S(2)}) collective-permute-start(f32[8,4]{1,0:T(8,128)S(1)} %broadcast_select_fusion), channel_id=1, source_target_pairs={{0,80},{16,96},{32,112},{48,0},{64,16},{80,32},{96,48},{112,64},{1... | collective-permute-start | bytes 392 | tf_op jit(solution)/shard_map/ppermute | solution.py:186
  65.8 5.5 %collective-permute-start.9 = (f32[8,4]{1,0:T(8,128)S(1)}, f32[8,4]{1,0:T(8,128)S(1)}, u32[]{:S(2)}, u32[]{:S(2)}) collective-permute-start(f32[8,4]{1,0:T(8,128)S(1)} %broadcast_select_fusion), channel_id=1, source_target_pairs={{0,64},{16,80},{32,96},{48,112},{64,0},{80,16},{96,32},{112,48},{1... | collective-permute-start | bytes 392 | tf_op jit(solution)/shard_map/ppermute | solution.py:186
  67.2 4.2 %collective-permute-start.8 = (f32[8,4]{1,0:T(8,128)S(1)}, f32[8,4]{1,0:T(8,128)S(1)}, u32[]{:S(2)}, u32[]{:S(2)}) collective-permute-start(f32[8,4]{1,0:T(8,128)S(1)} %broadcast_select_fusion), channel_id=1, source_target_pairs={{0,48},{16,64},{32,80},{48,96},{64,112},{80,0},{96,16},{112,32},{1... | collective-permute-start | bytes 392 | tf_op jit(solution)/shard_map/ppermute | solution.py:186
  69.2 4.0 %collective-permute-start.7 = (f32[8,4]{1,0:T(8,128)S(1)}, f32[8,4]{1,0:T(8,128)S(1)}, u32[]{:S(2)}, u32[]{:S(2)}) collective-permute-start(f32[8,4]{1,0:T(8,128)S(1)} %broadcast_select_fusion), channel_id=1, source_target_pairs={{0,32},{16,48},{32,64},{48,80},{64,96},{80,112},{96,0},{112,16},{1... | collective-permute-start | bytes 392 | tf_op jit(solution)/shard_map/ppermute | solution.py:186
  69.9 3.3 %collective-permute-start.6 = (f32[8,4]{1,0:T(8,128)S(1)}, f32[8,4]{1,0:T(8,128)S(1)}, u32[]{:S(2)}, u32[]{:S(2)}) collective-permute-start(f32[8,4]{1,0:T(8,128)S(1)} %broadcast_select_fusion), channel_id=1, source_target_pairs={{0,16},{16,32},{32,48},{48,64},{64,80},{80,96},{96,112},{112,0},{1... | collective-permute-start | bytes 392 | tf_op jit(solution)/shard_map/ppermute | solution.py:186
  74.1 1.3 %copy-start = (bf16[128,64,128]{2,1,0:T(8,128)(2,1)}, bf16[128,64,128]{2,1,0:T(8,128)(2,1)S(1)}, u32[]{:S(2)}) copy-start(bf16[128,64,128]{2,1,0:T(8,128)(2,1)S(1)} %all-to-all-done.got_ref) | copy-start | bytes 6291460

commit v2 on v1

v2 whole, which is shorter than its diff:
```python
import math

import jax
import jax.numpy as jnp
import numpy as np
from jax import lax
from jax.experimental import pallas as pl
from jax.experimental.pallas import tpu as pltpu
from jax.sharding import PartitionSpec as P

NT = (((1,), (1,)), ((), ()))


def tables():
    q = np.arange(32)
    k = np.arange(256)

    def rows(freq, conj):
        angle = 2.0 * np.pi / 4096.0 * ((freq[:, None] * k[None, :]) % 4096)
        c, s = np.cos(angle) / 64.0, np.sin(angle) / 64.0
        re = np.concatenate([c, s], 1)
        im = np.concatenate([-s, c], 1)
        return re, (-im if conj else im)

    def real_rows(freq, second):
        angle = 2.0 * np.pi / 4096.0 * ((freq[:, None] * k[None, :]) % 4096)
        c, s = np.cos(angle) / 64.0, np.sin(angle) / 64.0
        zero = np.zeros_like(c)
        pair = (zero, c), (zero, -s)
        if not second:
            pair = (c, zero), (-s, zero)
        return [np.concatenate(p, 1) for p in pair]

    first, other = [], []
    for high in (0, 1):
        n = 63 - q if high else q
        first += list(real_rows(16 * n, False))
        other += list(rows(16 * n, False))
    for high in (0, 1):
        n = 63 - q if high else q
        first += list(real_rows(8 + 16 * n, True))
        other += list(rows(-16 * (n + 1), True))
    whole = np.stack([np.concatenate(first, 0), np.concatenate(other, 0)]).astype(np.float32)
    hi = whole.astype(jnp.bfloat16)
    lo = (whole - hi.astype(np.float32)).astype(jnp.bfloat16)
    angle = 2.0 * np.pi / 4096.0 * (np.arange(8)[:, None] * k[None, :])
    twiddle = np.stack([np.cos(angle), -np.sin(angle)], 1).reshape(16, 256).astype(np.float32)
    return np.concatenate([hi, lo], 1), twiddle


def rfft(x):
    n = len(x)
    if n == 2:
        return [(x[0] + x[1], None), (x[0] - x[1], None)]
    even, odd = rfft(x[0::2]), rfft(x[1::2])
    out = [None] * (n // 2 + 1)
    out[0] = (even[0][0] + odd[0][0], None)
    out[n // 2] = (even[0][0] - odd[0][0], None)
    for b in range(1, n // 4 + 1):
        er, ei = even[b]
        dr, di = odd[b]
        if 4 * b == n:
            out[b] = (er, -dr)
            continue
        c, s = math.cos(2 * math.pi * b / n), -math.sin(2 * math.pi * b / n)
        if 8 * b == n:
            tr, ti = (dr + di) * c, (di - dr) * c
        else:
            tr, ti = dr * c - di * s, dr * s + di * c
        out[b] = (er + tr, ei + ti)
        out[n // 2 - b] = (er - tr, ti - ei)
    return out


STRIDE = 16


def natural_row(p_low):
    return p_low * 16 if STRIDE == 256 else p_low * 512


def rows_of(start):
    return pl.ds(start if isinstance(start, int) else pl.multiple_of(start, 16), 16)


def fourier_kernel(order_ref, image_ref, matrix_ref, twiddle_ref, out_ref, z_ref, natural_ref, square_ref):
    step = pl.program_id(0)

    def prepare(i, unit, totals):
        out = []
        for t in range(2):
            total = totals[t]
            at, to = rows_of(i * 16), rows_of(t * 128 + i * 16)
            for half in range(2):
                lanes = slice(half * 128, half * 128 + 128)
                x = [image_ref[t, at, b * 256 + half * 128 : b * 256 + half * 128 + 128] for b in range(16)]
                squares = [v * v for v in x]
                while len(squares) > 1:
                    squares = [u + v for u, v in zip(squares[0::2], squares[1::2])]
                total = total + squares[0]
                bins = rfft(x)

                def put(g, part, value):
                    hi = value.astype(jnp.bfloat16)
                    lo = (value - hi.astype(jnp.float32)).astype(jnp.bfloat16)
                    z_ref[unit, g, to, part * 256 + half * 128 : part * 256 + half * 128 + 128] = hi
                    z_ref[unit, g, to, 512 + part * 256 + half * 128 : 512 + part * 256 + half * 128 + 128] = lo

                put(0, 0, bins[0][0])
                put(0, 1, bins[8][0])
                for g in range(1, 8):
                    re, im = bins[g]
                    c = twiddle_ref[2 * g : 2 * g + 1, lanes]
                    s = twiddle_ref[2 * g + 1 : 2 * g + 2, lanes]
                    put(g, 0, re * c - im * s)
                    put(g, 1, re * s + im * c)
            out.append(total)
        return tuple(out)

    def transform(g, unit):
        kind = min(g, 1)
        both = lax.dot_general(matrix_ref[kind], z_ref[unit, g, :, :512], NT, preferred_element_type=jnp.float32)
        rest = lax.dot_general(matrix_ref[kind, :256], z_ref[unit, g, :, 512:], NT, preferred_element_type=jnp.float32)
        got = both[:256] + (both[256:] + rest)
        for which, residue in enumerate((g, 8 if g == 0 else 16 - g)):
            for w in range(2):
                low = 15 - residue if w else residue
                for c in range(2):
                    first = ((which * 2 + w) * 2 + c) * 32
                    for t in range(2):
                        row = low * 512 + w * 8 + c * 4 + unit * 2 + t
                        natural_ref[pl.ds(row, 32, stride=16), :] = got[first : first + 32, t * 128 : t * 128 + 128]

    def keep_squares(unit, totals):
        for t in range(2):
            square_ref[unit * 2 + t : unit * 2 + t + 1, :] = jnp.sum(totals[t], axis=0, keepdims=True)

    zero = jnp.zeros((16, 128), jnp.float32)

    @pl.when(step == 0)
    def _():
        keep_squares(0, lax.fori_loop(0, 8, lambda i, totals: prepare(i, 0, totals), (zero, zero)))

    @pl.when(step == 1)
    def _():
        totals = (zero, zero)
        for i in range(8):
            transform(i, 0)
            totals = prepare(i, 1, totals)
        keep_squares(1, totals)

    @pl.when(step == 2)
    def _():
        for g in range(8):
            transform(g, 1)
        sums = square_ref[...]
        high = sums.astype(jnp.bfloat16).astype(jnp.float32)
        tail = jnp.concatenate([high, sums - high], axis=0).astype(jnp.bfloat16)

        def place(d, carry):
            for u in range(4):
                p = order_ref[d * 4 + u]
                row = (p & 15) * 512 + lax.shift_right_logical(p, 4) * 16
                at = pl.multiple_of(row, 16)
                out_ref[d, u * 16 : u * 16 + 16, :] = natural_ref[pl.ds(at, 16), :].astype(jnp.bfloat16)
            out_ref[d, 64:72, :] = tail
            return carry

        lax.fori_loop(0, 128, place, 0, unroll=8)


def fourier(pair_order, images, matrix, twiddle):
    return pl.pallas_call(
        fourier_kernel,
        grid=(3,),
        out_shape=jax.ShapeDtypeStruct((128, 72, 128), jnp.bfloat16),
        in_specs=[
            pl.BlockSpec(memory_space=pltpu.SMEM),
            pl.BlockSpec((2, 128, 4096), lambda i: (jnp.minimum(i, 1), 0, 0)),
            pl.BlockSpec((2, 512, 512), lambda i: (0, 0, 0)),
            pl.BlockSpec((16, 256), lambda i: (0, 0)),
        ],
        out_specs=pl.BlockSpec((128, 72, 128), lambda i: (0, 0, 0)),
        scratch_shapes=[
            pltpu.VMEM((2, 8, 256, 1024), jnp.bfloat16),
            pltpu.VMEM((8192, 128), jnp.float32),
            pltpu.VMEM((4, 128), jnp.float32),
        ],
        compiler_params=pltpu.CompilerParams(vmem_limit_bytes=58 << 20),
        cost_estimate=pl.CostEstimate(flops=4 << 30, bytes_accessed=12 << 20, transcendentals=0),
    )(pair_order, images, matrix, twiddle)


PIECES = 4


def legendre_kernel(mine_ref, got_ref, legendre_ref, out_ref, weight_ref, column_ref, series_ref, in_sems, out_sems):
    def loads(slot):
        for piece in range(PIECES):
            rows = pl.ds(piece * 256, 257 if piece == PIECES - 1 else 256)
            yield pltpu.make_async_copy(legendre_ref.at[slot, rows], weight_ref.at[slot, rows], in_sems.at[slot, piece])

    def begin(slot):
        for copy in loads(slot):
            copy.start()

    begin(0)
    scales = []
    for block in range(8):
        total = got_ref[block * 16, 64:72, :].astype(jnp.float32)
        for band in range(1, 16):
            total = total + got_ref[block * 16 + band, 64:72, :].astype(jnp.float32)
        parts = jnp.sum(total, axis=1, keepdims=True)
        whole = parts + jnp.concatenate([parts[4:], parts[:4]], axis=0)
        scales.append(1.0 / jnp.sqrt(whole / 8388608.0 + 1e-6))
    for slot in range(4):
        for band in range(16):
            for block in range(8):
                column_ref[slot, block * 16 : block * 16 + 16, band * 128 : band * 128 + 128] = got_ref[
                    block * 16 + band, slot * 16 : slot * 16 + 16, :
                ]
    begin(1)

    def store(slot):
        return pltpu.make_async_copy(series_ref.at[slot], out_ref.at[slot], out_sems.at[slot])

    def work(slot, carry):
        @pl.when(slot < 2)
        def _():
            begin(slot + 2)

        for copy in loads(slot):
            copy.wait()
        product = lax.dot_general(weight_ref[slot], column_ref[slot], NT, preferred_element_type=jnp.float32)
        turned = jnp.transpose(product)
        keep = lax.broadcasted_iota(jnp.int32, (8, 1025), 1) <= 1023 - mine_ref[slot]
        for block in range(8):
            kept = jnp.where(keep, turned[block * 16 : block * 16 + 8], turned[block * 16 + 8 : block * 16 + 16])
            kept = kept * scales[block]
            series_ref[slot, block * 4 : block * 4 + 4, :] = kept[:4]
            series_ref[slot, 32 + block * 4 : 32 + block * 4 + 4, :] = kept[4:]
        store(slot).start()
        return carry

    lax.fori_loop(0, 4, work, 0)
    for slot in range(4):
        store(slot).wait()


def associated(mine, got, legendre):
    return pl.pallas_call(
        legendre_kernel,
        out_shape=jax.ShapeDtypeStruct((4, 64, 1025), jnp.float32),
        in_specs=[
            pl.BlockSpec(memory_space=pltpu.SMEM),
            pl.BlockSpec(memory_space=pltpu.VMEM),
            pl.BlockSpec(memory_space=pl.ANY),
        ],
        out_specs=pl.BlockSpec(memory_space=pl.ANY),
        scratch_shapes=[
            pltpu.VMEM((4, 1025, 2048), jnp.bfloat16),
            pltpu.VMEM((4, 128, 2048), jnp.bfloat16),
            pltpu.VMEM((4, 64, 1025), jnp.float32),
            pltpu.SemaphoreType.DMA((4, PIECES)),
            pltpu.SemaphoreType.DMA((4,)),
        ],
        compiler_params=pltpu.CompilerParams(vmem_limit_bytes=48 << 20),
        cost_estimate=pl.CostEstimate(flops=4 << 30, bytes_accessed=22 << 20, transcendentals=0),
    )(mine, got, legendre)


def shards(images, pair_order, legendre):
    matrix, twiddle = tables()
    message = fourier(pair_order, images, jnp.asarray(matrix), jnp.asarray(twiddle))
    axes = ("tm", "lata", "latb")
    got = lax.all_to_all(message, axes, split_axis=0, concat_axis=0, tiled=True)
    mine = lax.dynamic_slice_in_dim(pair_order, lax.axis_index(axes) * 4, 4)
    return jnp.transpose(associated(mine, got, legendre), (0, 2, 1))


def solution(mesh):
    in_specs = (P("tm", ("lata", "latb"), None), P(), P(("tm", "lata", "latb"), None, None))
    out_specs = P(("tm", "lata", "latb"), None, None)
    return jax.shard_map(shards, mesh=mesh, in_specs=in_specs, out_specs=out_specs, check_vma=False)
```

time: 87.4 us -> 66.9 us (0.77)
  starting transfers between devices: 33.1 us -> 11.5 us
  waiting for transfers between devices: 5.47 us -> 15.9 us
  Pallas kernels: 28.5 us -> 22.9 us
  local copies, waits for them, and re-layouts: 18.9 us -> 16.2 us
  other arithmetic: 0.97 us -> 0 us
    ppermute x13 -> x0, starting transfers between devices: 21.6 us -> none  [shifted(): lax.ppermute(value, axis, [(i, (i + by) % size) for i in range(size)])]
    all_to_all x1, waiting for transfers between devices: 0.01 us -> 15.9 us  [shards(): got = lax.all_to_all(message, axes, split_axis=0, concat_axis=0, tiled=True)]
    pallas_call x2, Pallas kernels: 28.5 us -> 22.9 us  [the longest x1 13.6 us: fourier(): pl.pallas_call(fourier_kernel, grid=(3,), out_shape=jax.ShapeDtypeStruct(...]
    ppermute x13 -> x0, waiting for transfers between devices: 5.47 us -> none  [shifted(): lax.ppermute(value, axis, [(i, (i + by) % size) for i in range(size)])]
    unnamed x3 -> x1, local copies, waits for them, and re-layouts: 16.8 us -> 15.5 us
  transfers between devices with their start and end apart: 14 -> 1, of which waited for: 4 -> 1; matrix products, arithmetic and copies ran while one was open for 21% -> 24% of each run, Pallas kernels for 0% -> 0%
where the time goes in v2:
time: 66.9 us; the launch traced here: 66.5 us
  Pallas kernels  22.9 us (34%)
  local copies, waits for them, and re-layouts  16.2 us (24%)
  waiting for transfers between devices  15.9 us (24%)
  starting transfers between devices  11.5 us (17%)
    all_to_all x1, waiting for transfers between devices, shards(): got = lax.all_to_all(message, axes, split_axis=0, concat_axis=0, tiled=True)  15.9 us
    unnamed x1, local copies, waits for them, and re-layouts  15.5 us
    pallas_call x1, Pallas kernels, fourier(): pl.pallas_call(fourier_kernel, grid=(3,), out_shape=jax.ShapeDtypeStruct(...  13.6 us
    all_to_all x1, starting transfers between devices, shards(): got = lax.all_to_all(message, axes, split_axis=0, concat_axis=0, tiled=True)  11.5 us
    pallas_call x1, Pallas kernels, associated(): pl.pallas_call(legendre_kernel, out_shape=jax.ShapeDtypeStruct((4, 64, 10...  9.34 us
  transfers between devices with their start and end apart: 1, of which 1 were waited for; matrix products, arithmetic and copies ran while one was open for 24% of the time, Pallas kernels for 0%

profile of v2, /device:TPU:1, one launch (start us, length us, event | category | flops | bytes accessed | tf_op | source)
XLA Modules:
  0.0 66.5 jit_solution(14801022372833514004)
XLA Ops:
  0.0 13.6 %shard_map.55 = bf16[128,72,128]{2,1,0:T(8,128)(2,1)} custom-call(s32[512]{0:T(512)} %order_ref.1, f32[4,128,4096]{2,1,0:T(8,128)} %image_ref.1, bf16[2,512,512]{2,1,0:T(8,128)(2,1)} %constant.25.clone.matrix_ref, f32[16,256]{1,0:T(8,128)} %constant.26.clone.twiddle_ref), custom_call_target="tpu_custom_call" | custom-call | flops 4294967296 | bytes 12582912 | tf_op jit(solution)/shard_map/pallas_call | solution.py:173
  13.6 11.5 %all-to-all-start = ((bf16[128,72,128]{2,1,0:T(8,128)(2,1)}), bf16[128,72,128]{2,1,0:T(8,128)(2,1)S(1)}, u32[]{:S(2)}, u32[]{:S(2)}) async-start(bf16[128,72,128]{2,1,0:T(8,128)(2,1)} %shard_map.55), calls=%async_computation | async-start | bytes 4718592 | tf_op jit(solution)/shard_map/all_to_all | solution.py:276
  25.1 0.8 %dynamic_slice.3.mine_ref = s32[4]{0:T(128)S(1)} dynamic-slice(s32[512]{0:T(512)} %order_ref.1, s32[]{:T(128)S(6)} %select_n.3), dynamic_slice_sizes={4} | dynamic-slice | bytes 36 | tf_op jit(solution)/shard_map/dynamic_slice | solution.py:277
  25.8 15.5 %copy.6.legendre_ref = bf16[4,1025,2048]{2,1,0:T(8,128)(2,1)} copy(bf16[4,1025,2048]{2,0,1:T(4,128)(2,1)} %param.7) | data formatting | bytes 33587200 | tf_op args[2]
  41.3 15.9 %all-to-all-done.got_ref = bf16[128,72,128]{2,1,0:T(8,128)(2,1)S(1)} async-done(((bf16[128,72,128]{2,1,0:T(8,128)(2,1)}), bf16[128,72,128]{2,1,0:T(8,128)(2,1)S(1)}, u32[]{:S(2)}, u32[]{:S(2)}) %all-to-all-start) | async-done | bytes 2359328 | tf_op jit(solution)/shard_map/all_to_all | solution.py:276
  57.2 9.3 %shard_map.56 = f32[4,64,1025]{2,1,0:T(8,128)} custom-call(s32[4]{0:T(128)S(1)} %dynamic_slice.3.mine_ref, bf16[128,72,128]{2,1,0:T(8,128)(2,1)S(1)} %all-to-all-done.got_ref, bf16[4,1025,2048]{2,1,0:T(8,128)(2,1)} %copy.6.legendre_ref), custom_call_target="tpu_custom_call" | custom-call | flops 4294967296 | bytes 23068672 | tf_op jit(solution)/shard_map/pallas_call | solution.py:251
Async XLA Ops:
  13.6 43.6 %all-to-all-start = ((bf16[128,72,128]{2,1,0:T(8,128)(2,1)}), bf16[128,72,128]{2,1,0:T(8,128)(2,1)S(1)}, u32[]{:S(2)}, u32[]{:S(2)}) async-start(bf16[128,72,128]{2,1,0:T(8,128)(2,1)} %shard_map.55), calls=%async_computation | async-start | bytes 4718592 | tf_op jit(solution)/shard_map/all_to_all | solution.py:276

commit v3 on v2

v3 whole, which is shorter than its diff:
```python
import math

import jax
import jax.numpy as jnp
import numpy as np
from jax import lax
from jax.experimental import pallas as pl
from jax.experimental.pallas import tpu as pltpu
from jax.sharding import PartitionSpec as P

NT = (((1,), (1,)), ((), ()))


def tables():
    q = np.arange(32)
    k = np.arange(256)

    def rows(freq, sign):
        angle = 2.0 * np.pi / 4096.0 * ((freq[:, None] * k[None, :]) % 4096)
        c, s = np.cos(angle) / 64.0, np.sin(angle) / 64.0
        zero = np.zeros_like(c)
        if sign == 0:
            return np.concatenate([c, zero], 1), np.concatenate([-s, zero], 1)
        if sign == 8:
            return np.concatenate([zero, c], 1), np.concatenate([zero, -s], 1)
        return np.concatenate([c, sign * s], 1), np.concatenate([-s, sign * c], 1)

    groups = []
    for g in range(8):
        first = []
        for residue, sign in ((g, 1 if g else 0), (16 - g if g else 8, -1 if g else 8)):
            for high in (0, 1):
                first += list(rows(residue + 16 * (63 - q if high else q), sign))
        groups.append(np.concatenate(first, 0))
    whole = np.stack(groups).astype(np.float32)
    hi = whole.astype(jnp.bfloat16)
    lo = (whole - hi.astype(np.float32)).astype(jnp.bfloat16)
    return np.concatenate([hi, lo], 1)


def rfft(x):
    n = len(x)
    if n == 2:
        return [(x[0] + x[1], None), (x[0] - x[1], None)]
    even, odd = rfft(x[0::2]), rfft(x[1::2])
    out = [None] * (n // 2 + 1)
    out[0] = (even[0][0] + odd[0][0], None)
    out[n // 2] = (even[0][0] - odd[0][0], None)
    for b in range(1, n // 4 + 1):
        er, ei = even[b]
        dr, di = odd[b]
        if 4 * b == n:
            out[b] = (er, -dr)
            continue
        c, s = math.cos(2 * math.pi * b / n), -math.sin(2 * math.pi * b / n)
        if 8 * b == n:
            tr, ti = (dr + di) * c, (di - dr) * c
        else:
            tr, ti = dr * c - di * s, dr * s + di * c
        out[b] = (er + tr, ei + ti)
        out[n // 2 - b] = (er - tr, ti - ei)
    return out


STRIDE = 16


def natural_row(p_low):
    return p_low * 16 if STRIDE == 256 else p_low * 512


def fourier_kernel(
    order_ref, image_ref, matrix_ref, out_ref, field_ref, rows_ref, za_ref, zb_ref, natural_ref, square_ref, message_ref, in_sems, row_sem, out_sems
):
    z_refs = (za_ref, zb_ref)

    def load(image, piece):
        rows = pl.ds(pl.multiple_of(piece * 16, 16), 16)
        return pltpu.make_async_copy(image_ref.at[image, rows], field_ref.at[image, rows], in_sems.at[image, piece])

    def begin(image):
        for piece in range(8):
            load(image, piece).start()

    matrix_load = pltpu.make_async_copy(matrix_ref, rows_ref, row_sem)

    def prepare(image):
        z_ref = z_refs[image // 2]

        def piece(i, total):
            load(image, i).wait()
            at = pl.ds(pl.multiple_of(i * 16, 16), 16)
            to = pl.ds(pl.multiple_of(image % 2 * 128 + i * 16, 16), 16)
            for half in range(2):
                x = [field_ref[image, at, b * 256 + half * 128 : b * 256 + half * 128 + 128] for b in range(16)]
                squares = [v * v for v in x]
                while len(squares) > 1:
                    squares = [u + v for u, v in zip(squares[0::2], squares[1::2])]
                total = total + squares[0]
                bins = rfft(x)
                pairs = [(bins[0][0], bins[8][0])] + bins[1:8]
                for g in range(8):
                    for part in range(2):
                        value = pairs[g][part]
                        hi = value.astype(jnp.bfloat16)
                        lo = (value - hi.astype(jnp.float32)).astype(jnp.bfloat16)
                        lane = part * 256 + half * 128
                        z_ref[g, to, lane : lane + 128] = hi
                        z_ref[g, to, 512 + lane : 512 + lane + 128] = lo
            return total

        total = lax.fori_loop(0, 8, piece, jnp.zeros((16, 128), jnp.float32), unroll=2)
        square_ref[image : image + 1, :] = jnp.sum(total, axis=0, keepdims=True)

    def transform(g, unit):
        z_ref = z_refs[unit]
        both = lax.dot_general(rows_ref[g], z_ref[g, :, :512], NT, preferred_element_type=jnp.float32)
        rest = lax.dot_general(rows_ref[g, :256], z_ref[g, :, 512:], NT, preferred_element_type=jnp.float32)
        got = both[:256] + (both[256:] + rest)
        for which, residue in enumerate((g, 16 - g if g else 8)):
            for w in range(2):
                low = 15 - residue if w else residue
                for c in range(2):
                    first = ((which * 2 + w) * 2 + c) * 32
                    for t in range(2):
                        row = low * 768 + w * 8 + c * 4 + unit * 2 + t
                        natural_ref[pl.ds(row, 32, stride=24), :] = got[first : first + 32, t * 128 : t * 128 + 128]

    for image in range(4):
        begin(image)
    matrix_load.start()
    prepare(0)
    prepare(1)
    prepare(2)
    prepare(3)
    matrix_load.wait()
    for g in range(8):
        transform(g, 0)
    for g in range(8):
        transform(g, 1)
    sums = square_ref[...]
    high = sums.astype(jnp.bfloat16).astype(jnp.float32)
    tail = jnp.concatenate([high, sums - high], axis=0).astype(jnp.bfloat16)

    def send(part):
        rows = pl.ds(part * 32, 32)
        return pltpu.make_async_copy(message_ref.at[rows], out_ref.at[rows], out_sems.at[part])

    for part in range(4):

        def place(d, carry):
            for u in range(4):
                p = order_ref[d * 4 + u]
                at = pl.multiple_of((p & 15) * 768 + lax.shift_right_logical(p, 4) * 24, 8)
                message_ref[d, u * 16 : u * 16 + 16, :] = natural_ref[pl.ds(at, 16), :].astype(jnp.bfloat16)
            message_ref[d, 64:72, :] = tail
            return carry

        lax.fori_loop(part * 32, part * 32 + 32, place, 0, unroll=8)
        send(part).start()
    for part in range(4):
        send(part).wait()


def fourier(pair_order, images, matrix):
    return pl.pallas_call(
        fourier_kernel,
        out_shape=jax.ShapeDtypeStruct((128, 72, 128), jnp.bfloat16),
        in_specs=[
            pl.BlockSpec(memory_space=pltpu.SMEM),
            pl.BlockSpec(memory_space=pl.ANY),
            pl.BlockSpec(memory_space=pl.ANY),
        ],
        out_specs=pl.BlockSpec(memory_space=pl.ANY),
        scratch_shapes=[
            pltpu.VMEM((4, 128, 4096), jnp.float32),
            pltpu.VMEM((8, 512, 512), jnp.bfloat16),
            pltpu.VMEM((8, 256, 1024), jnp.bfloat16),
            pltpu.VMEM((8, 256, 1024), jnp.bfloat16),
            pltpu.VMEM((12288, 128), jnp.float32),
            pltpu.VMEM((4, 128), jnp.float32),
            pltpu.VMEM((128, 72, 128), jnp.bfloat16),
            pltpu.SemaphoreType.DMA((4, 8)),
            pltpu.SemaphoreType.DMA,
            pltpu.SemaphoreType.DMA((4,)),
        ],
        compiler_params=pltpu.CompilerParams(vmem_limit_bytes=60 << 20),
        cost_estimate=pl.CostEstimate(flops=4 << 30, bytes_accessed=14 << 20, transcendentals=0),
    )(pair_order, images, matrix)


PIECES = 4


def legendre_kernel(mine_ref, got_ref, legendre_ref, out_ref, weight_ref, column_ref, series_ref, in_sems, out_sems):
    def loads(slot):
        for piece in range(PIECES):
            rows = pl.ds(piece * 256, 257 if piece == PIECES - 1 else 256)
            yield pltpu.make_async_copy(legendre_ref.at[slot, rows], weight_ref.at[slot, rows], in_sems.at[slot, piece])

    def begin(slot):
        for copy in loads(slot):
            copy.start()

    begin(0)
    scales = []
    for block in range(8):
        total = got_ref[block * 16, 64:72, :].astype(jnp.float32)
        for band in range(1, 16):
            total = total + got_ref[block * 16 + band, 64:72, :].astype(jnp.float32)
        parts = jnp.sum(total, axis=1, keepdims=True)
        whole = parts + jnp.concatenate([parts[4:], parts[:4]], axis=0)
        scales.append(1.0 / jnp.sqrt(whole / 8388608.0 + 1e-6))
    for slot in range(4):
        for band in range(16):
            for block in range(8):
                column_ref[slot, block * 16 : block * 16 + 16, band * 128 : band * 128 + 128] = got_ref[
                    block * 16 + band, slot * 16 : slot * 16 + 16, :
                ]
    begin(1)

    def store(slot):
        return pltpu.make_async_copy(series_ref.at[slot], out_ref.at[slot], out_sems.at[slot])

    def work(slot, carry):
        @pl.when(slot < 2)
        def _():
            begin(slot + 2)

        for copy in loads(slot):
            copy.wait()
        product = lax.dot_general(weight_ref[slot], column_ref[slot], NT, preferred_element_type=jnp.float32)
        turned = jnp.transpose(product)
        keep = lax.broadcasted_iota(jnp.int32, (8, 1025), 1) <= 1023 - mine_ref[slot]
        for block in range(8):
            kept = jnp.where(keep, turned[block * 16 : block * 16 + 8], turned[block * 16 + 8 : block * 16 + 16])
            kept = kept * scales[block]
            series_ref[slot, block * 4 : block * 4 + 4, :] = kept[:4]
            series_ref[slot, 32 + block * 4 : 32 + block * 4 + 4, :] = kept[4:]
        store(slot).start()
        return carry

    lax.fori_loop(0, 4, work, 0)
    for slot in range(4):
        store(slot).wait()


def associated(mine, got, legendre):
    return pl.pallas_call(
        legendre_kernel,
        out_shape=jax.ShapeDtypeStruct((4, 64, 1025), jnp.float32),
        in_specs=[
            pl.BlockSpec(memory_space=pltpu.SMEM),
            pl.BlockSpec(memory_space=pltpu.VMEM),
            pl.BlockSpec(memory_space=pl.ANY),
        ],
        out_specs=pl.BlockSpec(memory_space=pl.ANY),
        scratch_shapes=[
            pltpu.VMEM((4, 1025, 2048), jnp.bfloat16),
            pltpu.VMEM((4, 128, 2048), jnp.bfloat16),
            pltpu.VMEM((4, 64, 1025), jnp.float32),
            pltpu.SemaphoreType.DMA((4, PIECES)),
            pltpu.SemaphoreType.DMA((4,)),
        ],
        compiler_params=pltpu.CompilerParams(vmem_limit_bytes=48 << 20),
        cost_estimate=pl.CostEstimate(flops=4 << 30, bytes_accessed=22 << 20, transcendentals=0),
    )(mine, got, legendre)


def shards(images, pair_order, legendre):
    message = fourier(pair_order, images, jnp.asarray(tables()))
    axes = ("tm", "lata", "latb")
    got = lax.all_to_all(message, axes, split_axis=0, concat_axis=0, tiled=True)
    mine = lax.dynamic_slice_in_dim(pair_order, lax.axis_index(axes) * 4, 4)
    return jnp.transpose(associated(mine, got, legendre), (0, 2, 1))


def solution(mesh):
    in_specs = (P("tm", ("lata", "latb"), None), P(), P(("tm", "lata", "latb"), None, None))
    out_specs = P(("tm", "lata", "latb"), None, None)
    return jax.shard_map(shards, mesh=mesh, in_specs=in_specs, out_specs=out_specs, check_vma=False)
```

time: 66.9 us -> 64.5 us (0.964)
  Pallas kernels: 22.9 us -> 20.5 us
    pallas_call x1, Pallas kernels: 13.6 us -> 11.2 us  [fourier(): pl.pallas_call(fourier_kernel, out_shape=jax.ShapeDtypeStruct((128, 72, 1...]
  transfers between devices with their start and end apart: 1 -> 1, of which waited for: 1 -> 1; matrix products, arithmetic and copies ran while one was open for 24% -> 25% of each run, Pallas kernels for 0% -> 0%
where the time goes in v3:
time: 64.5 us; the launch traced here: 64.2 us
  Pallas kernels  20.5 us (32%)
  local copies, waits for them, and re-layouts  16.2 us (25%)
  waiting for transfers between devices  15.9 us (25%)
  starting transfers between devices  11.5 us (18%)
    all_to_all x1, waiting for transfers between devices, shards(): got = lax.all_to_all(message, axes, split_axis=0, concat_axis=0, tiled=True)  15.9 us
    unnamed x1, local copies, waits for them, and re-layouts  15.5 us
    all_to_all x1, starting transfers between devices, shards(): got = lax.all_to_all(message, axes, split_axis=0, concat_axis=0, tiled=True)  11.5 us
    pallas_call x1, Pallas kernels, fourier(): pl.pallas_call(fourier_kernel, out_shape=jax.ShapeDtypeStruct((128, 72, 1...  11.2 us
    pallas_call x1, Pallas kernels, associated(): pl.pallas_call(legendre_kernel, out_shape=jax.ShapeDtypeStruct((4, 64, 10...  9.34 us
  transfers between devices with their start and end apart: 1, of which 1 were waited for; matrix products, arithmetic and copies ran while one was open for 25% of the time, Pallas kernels for 0%

profile of v3, /device:TPU:1, one launch (start us, length us, event | category | flops | bytes accessed | tf_op | source)
XLA Modules:
  0.0 64.2 jit_solution(17985903788914988388)
XLA Ops:
  0.0 11.2 %shard_map.46 = bf16[128,72,128]{2,1,0:T(8,128)(2,1)} custom-call(s32[512]{0:T(512)} %order_ref.1, f32[4,128,4096]{2,1,0:T(8,128)} %image_ref.1, bf16[8,512,512]{2,1,0:T(8,128)(2,1)} %constant.23.clone.matrix_ref), custom_call_target="tpu_custom_call" | custom-call | flops 4294967296 | bytes 14680064 | tf_op jit(solution)/shard_map/pallas_call | solution.py:166
  11.2 11.5 %all-to-all-start = ((bf16[128,72,128]{2,1,0:T(8,128)(2,1)}), bf16[128,72,128]{2,1,0:T(8,128)(2,1)S(1)}, u32[]{:S(2)}, u32[]{:S(2)}) async-start(bf16[128,72,128]{2,1,0:T(8,128)(2,1)} %shard_map.46), calls=%async_computation | async-start | bytes 4718592 | tf_op jit(solution)/shard_map/all_to_all | solution.py:273
  22.7 0.8 %dynamic_slice.3.mine_ref = s32[4]{0:T(128)S(1)} dynamic-slice(s32[512]{0:T(512)} %order_ref.1, s32[]{:T(128)S(6)} %select_n.3), dynamic_slice_sizes={4} | dynamic-slice | bytes 36 | tf_op jit(solution)/shard_map/dynamic_slice | solution.py:274
  23.5 15.5 %copy.5.legendre_ref = bf16[4,1025,2048]{2,1,0:T(8,128)(2,1)} copy(bf16[4,1025,2048]{2,0,1:T(4,128)(2,1)} %param.6) | data formatting | bytes 33587200 | tf_op args[2]
  38.9 15.9 %all-to-all-done.got_ref = bf16[128,72,128]{2,1,0:T(8,128)(2,1)S(1)} async-done(((bf16[128,72,128]{2,1,0:T(8,128)(2,1)}), bf16[128,72,128]{2,1,0:T(8,128)(2,1)S(1)}, u32[]{:S(2)}, u32[]{:S(2)}) %all-to-all-start) | async-done | bytes 2359328 | tf_op jit(solution)/shard_map/all_to_all | solution.py:273
  54.8 9.3 %shard_map.47 = f32[4,64,1025]{2,1,0:T(8,128)} custom-call(s32[4]{0:T(128)S(1)} %dynamic_slice.3.mine_ref, bf16[128,72,128]{2,1,0:T(8,128)(2,1)S(1)} %all-to-all-done.got_ref, bf16[4,1025,2048]{2,1,0:T(8,128)(2,1)} %copy.5.legendre_ref), custom_call_target="tpu_custom_call" | custom-call | flops 4294967296 | bytes 23068672 | tf_op jit(solution)/shard_map/pallas_call | solution.py:249
Async XLA Ops:
  11.2 43.6 %all-to-all-start = ((bf16[128,72,128]{2,1,0:T(8,128)(2,1)}), bf16[128,72,128]{2,1,0:T(8,128)(2,1)S(1)}, u32[]{:S(2)}, u32[]{:S(2)}) async-start(bf16[128,72,128]{2,1,0:T(8,128)(2,1)} %shard_map.46), calls=%async_computation | async-start | bytes 4718592 | tf_op jit(solution)/shard_map/all_to_all | solution.py:273

commit v4 on v3

--- a/solution.py
+++ b/solution.py
@@ -138,7 +138,10 @@
         transform(g, 0)
     for g in range(8):
         transform(g, 1)
-    sums = square_ref[...]
+    lane = lax.broadcasted_iota(jnp.int32, (4, 128), 1)
+    image = lax.broadcasted_iota(jnp.int32, (4, 128), 0)
+    sums = jnp.sum(square_ref[...], axis=1, keepdims=True)
+    sums = jnp.sum(jnp.where(lane == image, sums, 0.0), axis=0, keepdims=True)
     high = sums.astype(jnp.bfloat16).astype(jnp.float32)
     tail = jnp.concatenate([high, sums - high], axis=0).astype(jnp.bfloat16)
 
@@ -152,8 +155,8 @@
             for u in range(4):
                 p = order_ref[d * 4 + u]
                 at = pl.multiple_of((p & 15) * 768 + lax.shift_right_logical(p, 4) * 24, 8)
-                message_ref[d, u * 16 : u * 16 + 16, :] = natural_ref[pl.ds(at, 16), :].astype(jnp.bfloat16)
-            message_ref[d, 64:72, :] = tail
+                message_ref[d, u * 8 : u * 8 + 8, :, :] = natural_ref[pl.ds(at, 16), :].astype(jnp.bfloat16).reshape(8, 2, 128)
+            message_ref[d, 32, :, :] = tail
             return carry
 
         lax.fori_loop(part * 32, part * 32 + 32, place, 0, unroll=8)
@@ -165,7 +168,7 @@
 def fourier(pair_order, images, matrix):
     return pl.pallas_call(
         fourier_kernel,
-        out_shape=jax.ShapeDtypeStruct((128, 72, 128), jnp.bfloat16),
+        out_shape=jax.ShapeDtypeStruct((128, 33, 2, 128), jnp.bfloat16),
         in_specs=[
             pl.BlockSpec(memory_space=pltpu.SMEM),
             pl.BlockSpec(memory_space=pl.ANY),
@@ -179,7 +182,7 @@
             pltpu.VMEM((8, 256, 1024), jnp.bfloat16),
             pltpu.VMEM((12288, 128), jnp.float32),
             pltpu.VMEM((4, 128), jnp.float32),
-            pltpu.VMEM((128, 72, 128), jnp.bfloat16),
+            pltpu.VMEM((128, 33, 2, 128), jnp.bfloat16),
             pltpu.SemaphoreType.DMA((4, 8)),
             pltpu.SemaphoreType.DMA,
             pltpu.SemaphoreType.DMA((4,)),
@@ -203,20 +206,22 @@
             copy.start()
 
     begin(0)
+    lanes = lax.broadcasted_iota(jnp.int32, (8, 128), 1)
+    images = lax.broadcasted_iota(jnp.int32, (8, 128), 0) & 3
     scales = []
     for block in range(8):
-        total = got_ref[block * 16, 64:72, :].astype(jnp.float32)
+        total = got_ref[block * 16, 32, :, :].astype(jnp.float32)
         for band in range(1, 16):
-            total = total + got_ref[block * 16 + band, 64:72, :].astype(jnp.float32)
-        parts = jnp.sum(total, axis=1, keepdims=True)
-        whole = parts + jnp.concatenate([parts[4:], parts[:4]], axis=0)
+            total = total + got_ref[block * 16 + band, 32, :, :].astype(jnp.float32)
+        both = jnp.broadcast_to(total[0:1] + total[1:2], (8, 128))
+        whole = jnp.sum(jnp.where(lanes == images, both, 0.0), axis=1, keepdims=True)
         scales.append(1.0 / jnp.sqrt(whole / 8388608.0 + 1e-6))
     for slot in range(4):
         for band in range(16):
             for block in range(8):
                 column_ref[slot, block * 16 : block * 16 + 16, band * 128 : band * 128 + 128] = got_ref[
-                    block * 16 + band, slot * 16 : slot * 16 + 16, :
-                ]
+                    block * 16 + band, slot * 8 : slot * 8 + 8, :, :
+                ].reshape(16, 128)
     begin(1)
 
     def store(slot):

time: 64.5 us -> 62.8 us (0.974)
  waiting for transfers between devices: 15.9 us -> 13.9 us
    all_to_all x1, waiting for transfers between devices: 15.9 us -> 13.9 us  [shards(): got = lax.all_to_all(message, axes, split_axis=0, concat_axis=0, tiled=True)]
  transfers between devices with their start and end apart: 1 -> 1, of which waited for: 1 -> 1; matrix products, arithmetic and copies ran while one was open for 25% -> 26% of each run, Pallas kernels for 0% -> 0%
where the time goes in v4:
time: 62.8 us; the launch traced here: 62.5 us
  Pallas kernels  20.8 us (33%)
  local copies, waits for them, and re-layouts  16.2 us (26%)
  waiting for transfers between devices  13.9 us (22%)
  starting transfers between devices  11.5 us (18%)
    unnamed x1, local copies, waits for them, and re-layouts  15.5 us
    all_to_all x1, waiting for transfers between devices, shards(): got = lax.all_to_all(message, axes, split_axis=0, concat_axis=0, tiled=True)  13.9 us
    pallas_call x1, Pallas kernels, fourier(): pl.pallas_call(fourier_kernel, out_shape=jax.ShapeDtypeStruct((128, 33, 2...  11.7 us
    all_to_all x1, starting transfers between devices, shards(): got = lax.all_to_all(message, axes, split_axis=0, concat_axis=0, tiled=True)  11.5 us
    pallas_call x1, Pallas kernels, associated(): pl.pallas_call(legendre_kernel, out_shape=jax.ShapeDtypeStruct((4, 64, 10...  9.15 us
  transfers between devices with their start and end apart: 1, of which 1 were waited for; matrix products, arithmetic and copies ran while one was open for 26% of the time, Pallas kernels for 0%

profile of v4, /device:TPU:1, one launch (start us, length us, event | category | flops | bytes accessed | tf_op | source)
XLA Modules:
  0.0 62.5 jit_solution(6424221766610949283)
XLA Ops:
  0.0 11.7 %shard_map.46 = bf16[128,33,2,128]{3,2,1,0:T(2,128)(2,1)} custom-call(s32[512]{0:T(512)} %order_ref.1, f32[4,128,4096]{2,1,0:T(8,128)} %image_ref.1, bf16[8,512,512]{2,1,0:T(8,128)(2,1)} %constant.23.clone.matrix_ref), custom_call_target="tpu_custom_call" | custom-call | flops 4294967296 | bytes 14680064 | tf_op jit(solution)/shard_map/pallas_call | solution.py:169
  11.7 11.5 %all-to-all-start = ((bf16[128,33,2,128]{3,2,1,0:T(2,128)(2,1)}), bf16[128,33,2,128]{3,2,1,0:T(2,128)(2,1)S(1)}, u32[]{:S(2)}, u32[]{:S(2)}) async-start(bf16[128,33,2,128]{3,2,1,0:T(2,128)(2,1)} %shard_map.46), calls=%async_computation | async-start | bytes 4325376 | tf_op jit(solution)/shard_map/all_to_all | solution.py:278
  23.2 0.8 %dynamic_slice.3.mine_ref = s32[4]{0:T(128)S(1)} dynamic-slice(s32[512]{0:T(512)} %order_ref.1, s32[]{:T(128)S(6)} %select_n.3), dynamic_slice_sizes={4} | dynamic-slice | bytes 36 | tf_op jit(solution)/shard_map/dynamic_slice | solution.py:279
  23.9 15.5 %copy.5.legendre_ref = bf16[4,1025,2048]{2,1,0:T(8,128)(2,1)} copy(bf16[4,1025,2048]{2,0,1:T(4,128)(2,1)} %param.6) | data formatting | bytes 33587200 | tf_op args[2]
  39.4 13.9 %all-to-all-done.got_ref = bf16[128,33,2,128]{3,2,1,0:T(2,128)(2,1)S(1)} async-done(((bf16[128,33,2,128]{3,2,1,0:T(2,128)(2,1)}), bf16[128,33,2,128]{3,2,1,0:T(2,128)(2,1)S(1)}, u32[]{:S(2)}, u32[]{:S(2)}) %all-to-all-start) | async-done | bytes 2162720 | tf_op jit(solution)/shard_map/all_to_all | solution.py:278
  53.3 9.2 %shard_map.47 = f32[4,64,1025]{2,1,0:T(8,128)} custom-call(s32[4]{0:T(128)S(1)} %dynamic_slice.3.mine_ref, bf16[128,33,2,128]{3,2,1,0:T(2,128)(2,1)S(1)} %all-to-all-done.got_ref, bf16[4,1025,2048]{2,1,0:T(8,128)(2,1)} %copy.5.legendre_ref), custom_call_target="tpu_custom_call" | custom-call | flops 4294967296 | bytes 23068672 | tf_op jit(solution)/shard_map/pallas_call | solution.py:254
Async XLA Ops:
  11.7 41.7 %all-to-all-start = ((bf16[128,33,2,128]{3,2,1,0:T(2,128)(2,1)}), bf16[128,33,2,128]{3,2,1,0:T(2,128)(2,1)S(1)}, u32[]{:S(2)}, u32[]{:S(2)}) async-start(bf16[128,33,2,128]{3,2,1,0:T(2,128)(2,1)} %shard_map.46), calls=%async_computation | async-start | bytes 4325376 | tf_op jit(solution)/shard_map/all_to_all | solution.py:278

commit v5 on v4

--- a/solution.py
+++ b/solution.py
@@ -70,7 +70,7 @@
 
 
 def fourier_kernel(
-    order_ref, image_ref, matrix_ref, out_ref, field_ref, rows_ref, za_ref, zb_ref, natural_ref, square_ref, message_ref, in_sems, row_sem, out_sems
+    pair_ref, image_ref, matrix_ref, out_ref, order_ref, field_ref, rows_ref, za_ref, zb_ref, natural_ref, square_ref, message_ref, in_sems, row_sem, order_sem, out_sems
 ):
     z_refs = (za_ref, zb_ref)
 
@@ -129,6 +129,8 @@
     for image in range(4):
         begin(image)
     matrix_load.start()
+    order_load = pltpu.make_async_copy(pair_ref, order_ref, order_sem)
+    order_load.start()
     prepare(0)
     prepare(1)
     prepare(2)
@@ -145,6 +147,8 @@
     high = sums.astype(jnp.bfloat16).astype(jnp.float32)
     tail = jnp.concatenate([high, sums - high], axis=0).astype(jnp.bfloat16)
 
+    order_load.wait()
+
     def send(part):
         rows = pl.ds(part * 32, 32)
         return pltpu.make_async_copy(message_ref.at[rows], out_ref.at[rows], out_sems.at[part])
@@ -170,12 +174,13 @@
         fourier_kernel,
         out_shape=jax.ShapeDtypeStruct((128, 33, 2, 128), jnp.bfloat16),
         in_specs=[
-            pl.BlockSpec(memory_space=pltpu.SMEM),
+            pl.BlockSpec(memory_space=pl.ANY),
             pl.BlockSpec(memory_space=pl.ANY),
             pl.BlockSpec(memory_space=pl.ANY),
         ],
         out_specs=pl.BlockSpec(memory_space=pl.ANY),
         scratch_shapes=[
+            pltpu.SMEM((512,), jnp.int32),
             pltpu.VMEM((4, 128, 4096), jnp.float32),
             pltpu.VMEM((8, 512, 512), jnp.bfloat16),
             pltpu.VMEM((8, 256, 1024), jnp.bfloat16),
@@ -184,6 +189,7 @@
             pltpu.VMEM((4, 128), jnp.float32),
             pltpu.VMEM((128, 33, 2, 128), jnp.bfloat16),
             pltpu.SemaphoreType.DMA((4, 8)),
+            pltpu.SemaphoreType.DMA,
             pltpu.SemaphoreType.DMA,
             pltpu.SemaphoreType.DMA((4,)),
         ],

time: 62.8 us -> 62.1 us (0.989)
  Pallas kernels: 20.8 us -> 20.1 us
    pallas_call x1, Pallas kernels: 11.7 us -> 11 us  [fourier(): pl.pallas_call(fourier_kernel, out_shape=jax.ShapeDtypeStruct((128, 33, 2...]
where the time goes in v5:
time: 62.1 us; the launch traced here: 61.8 us
  Pallas kernels  20.1 us (32%)
  local copies, waits for them, and re-layouts  16.2 us (26%)
  waiting for transfers between devices  13.9 us (22%)
  starting transfers between devices  11.5 us (19%)
    unnamed x1, local copies, waits for them, and re-layouts  15.5 us
    all_to_all x1, waiting for transfers between devices, shards(): got = lax.all_to_all(message, axes, split_axis=0, concat_axis=0, tiled=True)  13.9 us
    all_to_all x1, starting transfers between devices, shards(): got = lax.all_to_all(message, axes, split_axis=0, concat_axis=0, tiled=True)  11.5 us
    pallas_call x1, Pallas kernels, fourier(): pl.pallas_call(fourier_kernel, out_shape=jax.ShapeDtypeStruct((128, 33, 2...  11 us
    pallas_call x1, Pallas kernels, associated(): pl.pallas_call(legendre_kernel, out_shape=jax.ShapeDtypeStruct((4, 64, 10...  9.15 us
  transfers between devices with their start and end apart: 1, of which 1 were waited for; matrix products, arithmetic and copies ran while one was open for 26% of the time, Pallas kernels for 0%

profile of v5, /device:TPU:1, one launch (start us, length us, event | category | flops | bytes accessed | tf_op | source)
XLA Modules:
  0.0 61.8 jit_solution(5949490652858755474)
XLA Ops:
  0.0 11.0 %shard_map.46 = bf16[128,33,2,128]{3,2,1,0:T(2,128)(2,1)} custom-call(s32[512]{0:T(512)} %pair_ref.1, f32[4,128,4096]{2,1,0:T(8,128)} %image_ref.1, bf16[8,512,512]{2,1,0:T(8,128)(2,1)} %constant.23.clone.matrix_ref), custom_call_target="tpu_custom_call" | custom-call | flops 4294967296 | bytes 14680064 | tf_op jit(solution)/shard_map/pallas_call | solution.py:173
  11.0 11.5 %all-to-all-start = ((bf16[128,33,2,128]{3,2,1,0:T(2,128)(2,1)}), bf16[128,33,2,128]{3,2,1,0:T(2,128)(2,1)S(1)}, u32[]{:S(2)}, u32[]{:S(2)}) async-start(bf16[128,33,2,128]{3,2,1,0:T(2,128)(2,1)} %shard_map.46), calls=%async_computation | async-start | bytes 4325376 | tf_op jit(solution)/shard_map/all_to_all | solution.py:284
  22.5 0.8 %dynamic_slice.3.mine_ref = s32[4]{0:T(128)S(1)} dynamic-slice(s32[512]{0:T(512)} %pair_ref.1, s32[]{:T(128)S(6)} %select_n.3), dynamic_slice_sizes={4} | dynamic-slice | bytes 36 | tf_op jit(solution)/shard_map/dynamic_slice | solution.py:285
  23.3 15.5 %copy.5.legendre_ref = bf16[4,1025,2048]{2,1,0:T(8,128)(2,1)} copy(bf16[4,1025,2048]{2,0,1:T(4,128)(2,1)} %param.6) | data formatting | bytes 33587200 | tf_op args[2]
  38.8 13.9 %all-to-all-done.got_ref = bf16[128,33,2,128]{3,2,1,0:T(2,128)(2,1)S(1)} async-done(((bf16[128,33,2,128]{3,2,1,0:T(2,128)(2,1)}), bf16[128,33,2,128]{3,2,1,0:T(2,128)(2,1)S(1)}, u32[]{:S(2)}, u32[]{:S(2)}) %all-to-all-start) | async-done | bytes 2162720 | tf_op jit(solution)/shard_map/all_to_all | solution.py:284
  52.6 9.2 %shard_map.47 = f32[4,64,1025]{2,1,0:T(8,128)} custom-call(s32[4]{0:T(128)S(1)} %dynamic_slice.3.mine_ref, bf16[128,33,2,128]{3,2,1,0:T(2,128)(2,1)S(1)} %all-to-all-done.got_ref, bf16[4,1025,2048]{2,1,0:T(8,128)(2,1)} %copy.5.legendre_ref), custom_call_target="tpu_custom_call" | custom-call | flops 4294967296 | bytes 23068672 | tf_op jit(solution)/shard_map/pallas_call | solution.py:260
Async XLA Ops:
  11.0 41.7 %all-to-all-start = ((bf16[128,33,2,128]{3,2,1,0:T(2,128)(2,1)}), bf16[128,33,2,128]{3,2,1,0:T(2,128)(2,1)S(1)}, u32[]{:S(2)}, u32[]{:S(2)}) async-start(bf16[128,33,2,128]{3,2,1,0:T(2,128)(2,1)} %shard_map.46), calls=%async_computation | async-start | bytes 4325376 | tf_op jit(solution)/shard_map/all_to_all | solution.py:284

commit v6 on v5

--- a/solution.py
+++ b/solution.py
@@ -201,7 +201,7 @@
 PIECES = 4
 
 
-def legendre_kernel(mine_ref, got_ref, legendre_ref, out_ref, weight_ref, column_ref, series_ref, in_sems, out_sems):
+def legendre_kernel(pairs_ref, got_ref, legendre_ref, out_ref, mine_ref, weight_ref, column_ref, series_ref, mine_sem, in_sems, out_sems):
     def loads(slot):
         for piece in range(PIECES):
             rows = pl.ds(piece * 256, 257 if piece == PIECES - 1 else 256)
@@ -212,6 +212,8 @@
             copy.start()
 
     begin(0)
+    mine_load = pltpu.make_async_copy(pairs_ref, mine_ref, mine_sem)
+    mine_load.start()
     lanes = lax.broadcasted_iota(jnp.int32, (8, 128), 1)
     images = lax.broadcasted_iota(jnp.int32, (8, 128), 0) & 3
     scales = []
@@ -251,6 +253,7 @@
         store(slot).start()
         return carry
 
+    mine_load.wait()
     lax.fori_loop(0, 4, work, 0)
     for slot in range(4):
         store(slot).wait()
@@ -261,15 +264,17 @@
         legendre_kernel,
         out_shape=jax.ShapeDtypeStruct((4, 64, 1025), jnp.float32),
         in_specs=[
-            pl.BlockSpec(memory_space=pltpu.SMEM),
+            pl.BlockSpec(memory_space=pl.ANY),
             pl.BlockSpec(memory_space=pltpu.VMEM),
             pl.BlockSpec(memory_space=pl.ANY),
         ],
         out_specs=pl.BlockSpec(memory_space=pl.ANY),
         scratch_shapes=[
+            pltpu.SMEM((4,), jnp.int32),
             pltpu.VMEM((4, 1025, 2048), jnp.bfloat16),
             pltpu.VMEM((4, 128, 2048), jnp.bfloat16),
             pltpu.VMEM((4, 64, 1025), jnp.float32),
+            pltpu.SemaphoreType.DMA,
             pltpu.SemaphoreType.DMA((4, PIECES)),
             pltpu.SemaphoreType.DMA((4,)),
         ],

time: 62.1 us -> 61.6 us (level)
  no operation moved by 1% of the time
where the time goes in v6:
time: 61.6 us; the launch traced here: 61.3 us
  Pallas kernels  19.6 us (32%)
  local copies, waits for them, and re-layouts  16.2 us (26%)
  waiting for transfers between devices  13.9 us (23%)
  starting transfers between devices  11.5 us (19%)
    unnamed x1, local copies, waits for them, and re-layouts  15.5 us
    all_to_all x1, waiting for transfers between devices, shards(): got = lax.all_to_all(message, axes, split_axis=0, concat_axis=0, tiled=True)  13.9 us
    all_to_all x1, starting transfers between devices, shards(): got = lax.all_to_all(message, axes, split_axis=0, concat_axis=0, tiled=True)  11.5 us
    pallas_call x1, Pallas kernels, fourier(): pl.pallas_call(fourier_kernel, out_shape=jax.ShapeDtypeStruct((128, 33, 2...  11 us
    pallas_call x1, Pallas kernels, associated(): pl.pallas_call(legendre_kernel, out_shape=jax.ShapeDtypeStruct((4, 64, 10...  8.62 us
  transfers between devices with their start and end apart: 1, of which 1 were waited for; matrix products, arithmetic and copies ran while one was open for 26% of the time, Pallas kernels for 0%

profile of v6, /device:TPU:1, one launch (start us, length us, event | category | flops | bytes accessed | tf_op | source)
XLA Modules:
  0.0 61.3 jit_solution(17360198097486886771)
XLA Ops:
  0.0 11.0 %shard_map.46 = bf16[128,33,2,128]{3,2,1,0:T(2,128)(2,1)} custom-call(s32[512]{0:T(512)} %pair_ref.1, f32[4,128,4096]{2,1,0:T(8,128)} %image_ref.1, bf16[8,512,512]{2,1,0:T(8,128)(2,1)} %constant.23.clone.matrix_ref), custom_call_target="tpu_custom_call" | custom-call | flops 4294967296 | bytes 14680064 | tf_op jit(solution)/shard_map/pallas_call | solution.py:173
  11.0 11.5 %all-to-all-start = ((bf16[128,33,2,128]{3,2,1,0:T(2,128)(2,1)}), bf16[128,33,2,128]{3,2,1,0:T(2,128)(2,1)S(1)}, u32[]{:S(2)}, u32[]{:S(2)}) async-start(bf16[128,33,2,128]{3,2,1,0:T(2,128)(2,1)} %shard_map.46), calls=%async_computation | async-start | bytes 4325376 | tf_op jit(solution)/shard_map/all_to_all | solution.py:289
  22.5 0.8 %dynamic_slice.3.pairs_ref = s32[4]{0:T(128)S(1)} dynamic-slice(s32[512]{0:T(512)} %pair_ref.1, s32[]{:T(128)S(6)} %select_n.3), dynamic_slice_sizes={4} | dynamic-slice | bytes 36 | tf_op jit(solution)/shard_map/dynamic_slice | solution.py:290
  23.3 15.5 %copy.5.legendre_ref = bf16[4,1025,2048]{2,1,0:T(8,128)(2,1)} copy(bf16[4,1025,2048]{2,0,1:T(4,128)(2,1)} %param.6) | data formatting | bytes 33587200 | tf_op args[2]
  38.8 13.9 %all-to-all-done.got_ref = bf16[128,33,2,128]{3,2,1,0:T(2,128)(2,1)S(1)} async-done(((bf16[128,33,2,128]{3,2,1,0:T(2,128)(2,1)}), bf16[128,33,2,128]{3,2,1,0:T(2,128)(2,1)S(1)}, u32[]{:S(2)}, u32[]{:S(2)}) %all-to-all-start) | async-done | bytes 2162720 | tf_op jit(solution)/shard_map/all_to_all | solution.py:289
  52.6 8.6 %shard_map.47 = f32[4,64,1025]{2,1,0:T(8,128)} custom-call(s32[4]{0:T(128)S(1)} %dynamic_slice.3.pairs_ref, bf16[128,33,2,128]{3,2,1,0:T(2,128)(2,1)S(1)} %all-to-all-done.got_ref, bf16[4,1025,2048]{2,1,0:T(8,128)(2,1)} %copy.5.legendre_ref), custom_call_target="tpu_custom_call" | custom-call | flops 4294967296 | bytes 23068672 | tf_op jit(solution)/shard_map/pallas_call | solution.py:263
Async XLA Ops:
  11.0 41.7 %all-to-all-start = ((bf16[128,33,2,128]{3,2,1,0:T(2,128)(2,1)}), bf16[128,33,2,128]{3,2,1,0:T(2,128)(2,1)S(1)}, u32[]{:S(2)}, u32[]{:S(2)}) async-start(bf16[128,33,2,128]{3,2,1,0:T(2,128)(2,1)} %shard_map.46), calls=%async_computation | async-start | bytes 4325376 | tf_op jit(solution)/shard_map/all_to_all | solution.py:289
